TPU v7x, 128 devices: a whole 4x4x4 slice. The times are simulated.
128 devices in a mesh: lat: 8 (over x_lo, z), lon: 16 (over x_hi, y, core).
Axes of the slice: x: 4 (x_hi: 2, x_lo: 2; x = x_hi * 2 + x_lo), y: 4, z: 4, core: 2. Of those that a mesh axis runs over, the one named last changes fastest.
Arguments:
- tokens: bfloat16 [4, 48, 384, 512], P(None, 'lat', 'lon'), may hold values from -6 to 6
- cotangent: bfloat16 [4, 48, 384, 512], P(None, 'lat', 'lon'), may hold values from -6 to 6
- region_ids: int32 [4, 48, 384], P(None, 'lat', 'lon'), may hold values from 0 to 3
- norm_gain: float32 [512], replicated, may hold values from 0.1 to 1.9
- qkv_weight: bfloat16 [512, 1536], replicated
- out_weight: bfloat16 [512, 512], replicated, may hold values from -0.25 to 0.25
Outputs:
- result: bfloat16 [4, 48, 384, 512], P(None, 'lat', 'lon')
- grad_input: bfloat16 [4, 48, 384, 512], P(None, 'lat', 'lon')
- grad_qkv: float32 [512, 1536], P('lat', 'lon')
- grad_out: float32 [512, 512], P('lat', 'lon')
All inputs are finite; a program needn't handle non-finite values.
Results may differ from a plain program's by a relative error of at most 0.0059.
The roundings to bfloat16 on the way count: a program that leaves them out, or rounds other values in their place, can miss the bound.
Values may be sent and summed in bfloat16 or wider, within the bound.
A program may use at most 128 MiB of HBM per device.

v0:
```python
import jax
import jax.numpy as jnp
from jax import lax
import numpy as np
from jax.experimental import pallas as pl
from jax.experimental.pallas import tpu as pltpu
from jax.sharding import PartitionSpec as P

SPAN = 144
NN = (((1,), (0,)), ((), ()))
NT = (((1,), (1,)), ((), ()))
BF = jnp.bfloat16
F32 = jnp.float32


def from_behind(array, axis, by):
    count = lax.axis_size(axis)
    return lax.ppermute(array, axis, [(i, (i + by) % count) for i in range(count)])


def window_split(array):
    levels, rows, columns = array.shape[:3]
    rest = array.shape[3:]
    sectioned = array.reshape((levels // 2, 2, rows // 6, 6, columns // 12, 12) + rest)
    order = (0, 2, 4, 1, 3, 5) + tuple(range(6, 6 + len(rest)))
    sectioned = sectioned.transpose(order)
    return sectioned.reshape((levels // 2 * (rows // 6) * (columns // 12), 144) + rest)


def window_join(array, levels, rows, columns):
    rest = array.shape[2:]
    sectioned = array.reshape((levels // 2, rows // 6, columns // 12, 2, 6, 12) + rest)
    order = (0, 3, 1, 4, 2, 5) + tuple(range(6, 6 + len(rest)))
    return sectioned.transpose(order).reshape((levels, rows, columns) + rest)


def roll_ahead(block):
    block = jnp.roll(block, 1, 0)
    came = from_behind(block[:, -3:], "lat", 1)
    block = jnp.concatenate([came, block[:, :-3]], 1)
    came = from_behind(block[:, :, -6:], "lon", 1)
    return jnp.concatenate([came, block[:, :, :-6]], 2)


def roll_behind(block):
    block = jnp.roll(block, -1, 0)
    came = from_behind(block[:, :3], "lat", -1)
    block = jnp.concatenate([block[:, 3:], came], 1)
    came = from_behind(block[:, :, :6], "lon", -1)
    return jnp.concatenate([block[:, :, 6:], came], 2)


def dot(a, b, dims=NN):
    return lax.dot_general(a, b, dims, preferred_element_type=F32)


def compute_kernel(x_ref, cot_ref, hot_ref, gain_ref, w_ref, wo_ref, eye_ref,
                   out_ref, gs_ref, gqkv_ref, gout_ref,
                   normed_ref, nbf_ref, inv_ref, proj_ref, att_ref, ga_ref, gp_ref, tr_ref):
    tokens, width = x_ref.shape
    windows = tokens // SPAN
    gain = gain_ref[...]
    for w in range(windows):
        rows = pl.ds(w * SPAN, SPAN)
        x = x_ref[rows, :].astype(F32)
        centered = x - jnp.mean(x, -1, keepdims=True)
        var = jnp.mean(centered * centered, -1, keepdims=True)
        inv = lax.rsqrt(var + 1e-5)
        normed = centered * inv
        normed_ref[rows, :] = normed
        inv_ref[rows, :] = inv
        nbf_ref[rows, :] = (normed * gain).astype(BF)
    for c in range(6):
        cols = pl.ds(c * 256, 256)
        proj_ref[:, cols] = dot(nbf_ref[...], w_ref[:, cols]).astype(BF)
    for c in range(2):
        ga_ref[:, pl.ds(c * 256, 256)] = dot(cot_ref[...], wo_ref[pl.ds(c * 256, 256), :], NT).astype(BF)

    lane = lax.broadcasted_iota(jnp.int32, (1, 128), 1)
    masks = [jnp.where((lane < 64) == (h == 0), 1.0, 0.0).astype(BF) for h in range(2)]
    eighths = [(m * 0.125).astype(BF) for m in masks]
    eye = eye_ref[...]
    eye128 = eye_ref[:128, :128]

    def pair(p, _):
        at = pl.multiple_of(p * 128, 128)
        for w in range(windows):
            rows = pl.ds(w * SPAN, SPAN)
            q2 = proj_ref[rows, pl.ds(at, 128)]
            k2 = proj_ref[rows, pl.ds(pl.multiple_of(512 + at, 128), 128)]
            v2 = proj_ref[rows, pl.ds(pl.multiple_of(1024 + at, 128), 128)]
            g2 = ga_ref[rows, pl.ds(at, 128)]
            hot = hot_ref[rows, :]
            qx = jnp.concatenate([q2, hot * jnp.array(-1e30, BF)], 1)
            off = (1.0 - hot.astype(F32)).astype(BF)
            qt = dot(eye128, q2 * jnp.array(0.125, BF), NT).astype(BF)
            gt = dot(eye128, g2, NT).astype(BF)
            att = []
            gq = None
            gkt = []
            gvt = []
            for h in range(2):
                kh = k2 * eighths[h]
                s = dot(qx, jnp.concatenate([kh, off], 1), NT)
                m = jnp.max(s, -1, keepdims=True)
                e = jnp.exp(s - m)
                a = e * (1.0 / jnp.sum(e, -1, keepdims=True))
                abf = a.astype(BF)
                att.append(dot(abf, v2))
                gw = dot(g2, v2 * masks[h], NT)
                prod = gw * a
                inner = jnp.sum(prod, -1, keepdims=True)
                ds = (prod - a * inner).astype(BF)
                part = dot(ds, kh)
                gq = part if gq is None else gq + part
                gkt.append(dot(qt[64 * h:64 * h + 64], ds))
                gvt.append(dot(gt[64 * h:64 * h + 64], abf))
            att_ref[rows, pl.ds(at, 128)] = jnp.where(lane < 64, att[0], att[1]).astype(BF)
            gp_ref[rows, pl.ds(at, 128)] = gq.astype(BF)
            gk = dot(eye, jnp.concatenate(gkt, 0).astype(BF), NT)
            gv = dot(eye, jnp.concatenate(gvt, 0).astype(BF), NT)
            gp_ref[rows, pl.ds(pl.multiple_of(512 + at, 128), 128)] = gk.astype(BF)
            gp_ref[rows, pl.ds(pl.multiple_of(1024 + at, 128), 128)] = gv.astype(BF)
        return 0

    lax.fori_loop(0, 4, pair, 0)

    for w in range(windows):
        rows = pl.ds(w * SPAN, SPAN)
        branch = dot(att_ref[rows, :], wo_ref[...])
        out_ref[rows, :] = (x_ref[rows, :].astype(F32) + branch).astype(BF)
        gh = dot(gp_ref[rows, :], w_ref[...], NT) * gain
        normed = normed_ref[rows, :]
        gs = inv_ref[rows, :] * (gh - jnp.mean(gh, -1, keepdims=True)
                                 - normed * jnp.mean(gh * normed, -1, keepdims=True))
        gs_ref[rows, :] = gs.astype(BF)
    tr_ref[...] = nbf_ref[...].T
    for c in range(6):
        cols = pl.ds(c * 256, 256)
        gqkv_ref[:, cols] = dot(tr_ref[...], gp_ref[:, cols])
    tr_ref[...] = att_ref[...].T
    for c in range(2):
        cols = pl.ds(c * 256, 256)
        gout_ref[:, cols] = dot(tr_ref[...], cot_ref[:, cols])


def compute(x, cot, hot, gain, w, wo):
    tokens, width = x.shape
    eye = jnp.asarray(np.eye(SPAN), BF)
    vm = pl.BlockSpec(memory_space=pltpu.VMEM)
    return pl.pallas_call(
        compute_kernel,
        out_shape=(
            jax.ShapeDtypeStruct((tokens, width), BF),
            jax.ShapeDtypeStruct((tokens, width), BF),
            jax.ShapeDtypeStruct((width, 3 * width), F32),
            jax.ShapeDtypeStruct((width, width), F32),
        ),
        in_specs=[vm] * 7,
        out_specs=(vm,) * 4,
        scratch_shapes=[
            pltpu.VMEM((tokens, width), F32),
            pltpu.VMEM((tokens, width), BF),
            pltpu.VMEM((tokens, 1), F32),
            pltpu.VMEM((tokens, 3 * width), BF),
            pltpu.VMEM((tokens, width), BF),
            pltpu.VMEM((tokens, width), BF),
            pltpu.VMEM((tokens, 3 * width), BF),
            pltpu.VMEM((width, tokens), BF),
        ],
        compiler_params=pltpu.CompilerParams(vmem_limit_bytes=48 << 20),
    )(x, cot, hot, gain, w, wo, eye)


def on_device(tokens, cotangent, region_ids, norm_gain, qkv_weight, out_weight):
    levels, rows, columns, width = tokens.shape
    rolled = roll_ahead(jnp.concatenate([tokens, cotangent], -1))
    shifted = window_split(rolled[..., :width])
    shifted_cot = window_split(rolled[..., width:])
    region = window_split(region_ids)
    hot = (region.reshape(-1, 1) == jnp.arange(128)[None]).astype(BF)
    shifted_out, grad_shifted, grad_qkv, grad_out = compute(
        shifted.reshape(-1, width), shifted_cot.reshape(-1, width), hot, norm_gain.reshape(1, -1), qkv_weight, out_weight
    )
    shifted_out, grad_shifted = shifted_out.reshape(4, SPAN, width), grad_shifted.reshape(4, SPAN, width)
    joined = jnp.concatenate(
        [
            window_join(shifted_out, levels, rows, columns),
            window_join(grad_shifted, levels, rows, columns),
        ],
        -1,
    )
    returned = roll_behind(joined)
    result = returned[..., :width]
    grad_input = (cotangent.astype(jnp.float32) + returned[..., width:].astype(jnp.float32)).astype(
        jnp.bfloat16
    )
    first_qkv, first_out = (
        lax.psum_scatter(grad_qkv, "lat", scatter_dimension=0, tiled=True),
        lax.psum_scatter(grad_out, "lat", scatter_dimension=0, tiled=True),
    )
    owned_qkv, owned_out = (
        lax.psum_scatter(first_qkv, "lon", scatter_dimension=1, tiled=True),
        lax.psum_scatter(first_out, "lon", scatter_dimension=1, tiled=True),
    )
    return (result, grad_input, owned_qkv, owned_out)


def solution(mesh):
    placed = (
        P(None, "lat", "lon", None),
        P(None, "lat", "lon", None),
        P(None, "lat", "lon"),
        P(),
        P(),
        P(),
    )
    return jax.shard_map(
        on_device,
        mesh=mesh,
        in_specs=placed,
        out_specs=(
            P(None, "lat", "lon", None),
            P(None, "lat", "lon", None),
            P("lat", "lon"),
            P("lat", "lon"),
        ),
        check_vma=False,
    )
```

profile of v0, /device:TPU:1, one launch (start us, length us, event | category | flops | bytes accessed | tf_op | source)
XLA Modules:
  0.0 299.8 jit_solution(9781937885459877859)
XLA Ops:
  7.2 0.0 reduce-scatter.9.cloned.1.call-start
  7.2 1.2 constant_dynamic-update-slice_fusion.1
  8.4 0.1 constant_dynamic-update-slice_fusion
  8.5 0.1 slice.69
  8.6 0.1 fusion.4
  8.7 0.0 copy-start.8
  8.7 2.5 collective-permute-start
  11.2 16.1 %collective-permute-done = bf16[4,3,24,1024]{3,2,1,0:T(8,128)(2,1)S(1)} collective-permute-done((bf16[4,3,24,1024]{3,2,1,0:T(8,128)(2,1)S(1)}, bf16[4,3,24,1024]{3,2,1,0:T(8,128)(2,1)S(1)}, u32[]{:S(2)}, u32[]{:S(2)}) %collective-permute-start) | collective-permute-done | bytes 589856 | tf_op jit(solution)/shard_map/ppermute | solution.py:18
  27.3 0.1 pad_maximum_fusion.4
  27.4 2.5 collective-permute-start.1
  29.9 0.1 reshape.29
  30.0 0.1 eq.15
  30.1 0.1 fusion.5.hot_ref
  30.3 4.4 %collective-permute-done.1 = bf16[4,6,6,1024]{3,2,1,0:T(8,128)(2,1)S(1)} collective-permute-done((bf16[4,6,6,1024]{3,2,1,0:T(8,128)(2,1)S(1)}, bf16[4,6,6,1024]{3,2,1,0:T(8,128)(2,1)S(1)}, u32[]{:S(2)}, u32[]{:S(2)}) %collective-permute-start.1) | collective-permute-done | bytes 294944 | tf_op jit(solution)/shard_map/ppermute | solution.py:18
  34.6 0.5 fusion
  35.2 0.1 fusion.6
  35.3 0.5 copy.29
  35.8 0.2 reshape.28
  36.0 0.1 copy.30
  36.1 0.1 reshape_reshape.14.cot_ref
  36.3 0.5 copy.27
  36.7 0.2 reshape.27
  37.0 0.0 copy-start.5
  37.0 1.1 copy.28
  38.1 1.3 reshape_reshape.13.x_ref
  39.3 1.0 copy-done.3
  40.4 0.9 copy-done.4
  41.3 20.7 %shard_map.102 = (bf16[576,512]{1,0:T(8,128)(2,1)S(1)}, bf16[576,512]{1,0:T(8,128)(2,1)S(1)}, f32[512,1536]{1,0:T(8,128)}, f32[512,512]{1,0:T(8,128)}) custom-call(bf16[576,512]{1,0:T(8,128)(2,1)S(1)} %reshape_reshape.13.x_ref, bf16[576,512]{1,0:T(8,128)(2,1)S(1)} %reshape_reshape.14.cot_ref, bf16[576,128]{1,0:T(8,128)(2,1)S(1)} %fusion.5.hot_ref, ...), custom_call_target="tpu_custom_call" | custom-call | tf_op jit(solution)/shard_map/pallas_call | solution.py:151
  61.9 0.8 copy-done.1
  62.8 0.0 reduce-scatter.9.cloned.1.call-update
  62.8 0.0 reduce-scatter.11.cloned.1.call-start
  62.8 0.7 reduce-scatter.11.cloned.1.call-update
  63.5 0.2 reduce-scatter.13.cloned.1.call-start
  63.8 0.1 copy-done.2
  63.9 0.1 reshape_reshape.15
  64.0 0.6 copy.32
  64.6 0.2 reshape.31
  64.8 0.1 reshape_reshape.16
  65.0 0.6 copy.33
  65.6 0.2 reshape.32
  65.8 0.2 constant_dynamic-update-slice_fusion.3
  66.1 0.3 constant_dynamic-update-slice_fusion.2
  66.3 0.4 slice.75
  66.7 0.6 slice.74
  67.4 1.2 pad_maximum_fusion.3
  68.6 1.5 collective-permute-start.2
  70.1 45.2 %reduce-scatter.9.cloned.1.call-done = f32[64,1536]{1,0:T(8,128)} async-done(((f32[512,1536]{1,0:T(8,128)}), f32[64,1536]{1,0:T(8,128)}) %reduce-scatter.9.cloned.1.call-update) | async-done | bytes 393232 | tf_op jit(solution)/shard_map/reduce_scatter | solution.py:199
  115.4 2.2 copy.38
  117.5 0.0 reduce-scatter.13.cloned.1.call-update
  117.6 0.0 reduce-scatter.15.cloned.1.call-start
  117.6 0.2 pad_maximum_fusion.5
  117.8 2.6 collective-permute-start.3
  120.4 0.6 fusion.1
  121.0 4.8 %collective-permute-done.3 = bf16[4,6,6,1024]{3,0,2,1:T(4,128)(2,1)S(1)} collective-permute-done((bf16[4,6,6,1024]{3,0,2,1:T(4,128)(2,1)S(1)}, bf16[4,6,6,1024]{3,0,2,1:T(4,128)(2,1)S(1)}, u32[]{:S(2)}, u32[]{:S(2)}) %collective-permute-start.3) | collective-permute-done | bytes 294944 | tf_op jit(solution)/shard_map/ppermute | solution.py:18
  125.8 0.4 fusion.2
  126.2 0.9 copy.35
  127.1 26.1 %reduce-scatter.11.cloned.1.call-done = f32[64,512]{1,0:T(8,128)} async-done(((f32[512,512]{1,0:T(8,128)}), f32[64,512]{1,0:T(8,128)}) %reduce-scatter.11.cloned.1.call-update) | async-done | bytes 131088 | tf_op jit(solution)/shard_map/reduce_scatter | solution.py:200
  153.2 1.7 copy.40
  155.0 0.0 reduce-scatter.15.cloned.1.call-update
  155.0 0.6 add_convert_fusion
  155.6 0.9 copy.36
  156.5 68.1 %reduce-scatter.13.cloned.1.call-done = f32[96,64]{1,0:T(8,128)} async-done(((f32[1536,64]{1,0:T(8,128)}), f32[96,64]{1,0:T(8,128)}) %reduce-scatter.13.cloned.1.call-update) | async-done | bytes 24592
  224.7 1.5 copy.39
  226.2 67.1 %reduce-scatter.15.cloned.1.call-done = f32[32,64]{1,0:T(8,128)} async-done(((f32[512,64]{1,0:T(8,128)}), f32[32,64]{1,0:T(8,128)}) %reduce-scatter.15.cloned.1.call-update) | async-done | bytes 8208
  (15 shorter events, 0.1 us)
Async XLA Ops:
  7.2 1.3 copy-start.6
  7.2 108.2 %reduce-scatter.9.cloned.1.call-start = ((), (), s32[]{:S(2)}) async-start(), calls=%async_computation.4 | async-start | bytes 3538944 | tf_op jit(solution)/shard_map/reduce_scatter | solution.py:199
  8.7 21.2 %copy-start.8 = (s32[4,6,24]{2,0,1:T(4,128)S(1)}, s32[4,6,24]{2,0,1:T(4,128)}, u32[]{:S(2)}) copy-start(s32[4,6,24]{2,0,1:T(4,128)} %param.9) | copy-start | bytes 6916
  8.7 18.6 %collective-permute-start = (bf16[4,3,24,1024]{3,2,1,0:T(8,128)(2,1)S(1)}, bf16[4,3,24,1024]{3,2,1,0:T(8,128)(2,1)S(1)}, u32[]{:S(2)}, u32[]{:S(2)}) collective-permute-start(bf16[4,3,24,1024]{3,2,1,0:T(8,128)(2,1)S(1)} %fusion.4), channel_id=1, source_target_pairs={{0,16},{16,32},{32,48},{48,64},{64,80},{80,96},{96,112},{112,0},{1... | collective-permute-start | bytes 1769480 | tf_op jit(solution)/shard_map/ppermute | solution.py:18
  27.4 7.2 %collective-permute-start.1 = (bf16[4,6,6,1024]{3,2,1,0:T(8,128)(2,1)S(1)}, bf16[4,6,6,1024]{3,2,1,0:T(8,128)(2,1)S(1)}, u32[]{:S(2)}, u32[]{:S(2)}) collective-permute-start(bf16[4,6,6,1024]{3,2,1,0:T(8,128)(2,1)S(1)} %pad_maximum_fusion.4), channel_id=1, source_target_pairs={{0,1},{1,2},{2,3},{3,4},{4,5},{5,6},{6,7},{7,8},{8,9},{9,10},{10,1... | collective-permute-start | bytes 884744 | tf_op jit(solution)/shard_map/ppermute | solution.py:18
  37.0 2.3 copy-start
  37.0 2.3 copy-start.5
  39.3 1.0 copy-start.3
  40.4 0.9 copy-start.4
  61.9 0.8 copy-start.1
  62.8 1.1 copy-start.2
  62.8 90.4 %reduce-scatter.11.cloned.1.call-start = ((), (), s32[]{:S(2)}) async-start(), calls=%async_computation.5 | async-start | bytes 1179648 | tf_op jit(solution)/shard_map/reduce_scatter | solution.py:200
  63.5 161.1 %reduce-scatter.13.cloned.1.call-start = ((), (), s32[]{:S(2)}) async-start(), calls=%async_computation.6 | async-start | bytes 835584
  68.6 49.0 %collective-permute-start.2 = (bf16[4,3,24,1024]{3,0,2,1:T(4,128)(2,1)S(1)}, bf16[4,3,24,1024]{3,0,2,1:T(4,128)(2,1)S(1)}, u32[]{:S(2)}, u32[]{:S(2)}) collective-permute-start(bf16[4,3,24,1024]{3,0,2,1:T(4,128)(2,1)S(1)} %get-tuple-element.24), channel_id=1, source_target_pairs={{0,112},{16,0},{32,16},{48,32},{64,48},{80,64},{96,80},{112,96},{1... | collective-permute-start | bytes 1769480 | tf_op jit(solution)/shard_map/ppermute | solution.py:18
  117.6 175.7 %reduce-scatter.15.cloned.1.call-start = ((), (), s32[]{:S(2)}) async-start(), calls=%async_computation.7 | async-start | bytes 278528
  117.8 8.0 %collective-permute-start.3 = (bf16[4,6,6,1024]{3,0,2,1:T(4,128)(2,1)S(1)}, bf16[4,6,6,1024]{3,0,2,1:T(4,128)(2,1)S(1)}, u32[]{:S(2)}, u32[]{:S(2)}) collective-permute-start(bf16[4,6,6,1024]{3,0,2,1:T(4,128)(2,1)S(1)} %pad_maximum_fusion.5), channel_id=1, source_target_pairs={{0,15},{1,0},{2,1},{3,2},{4,3},{5,4},{6,5},{7,6},{8,7},{9,8},{10,9... | collective-permute-start | bytes 884744 | tf_op jit(solution)/shard_map/ppermute | solution.py:18
  126.2 28.8 %copy-start.7 = (bf16[4,6,24,512]{3,2,1,0:T(8,128)(2,1)S(1)}, bf16[4,6,24,512]{3,2,1,0:T(8,128)(2,1)}, u32[]{:S(2)}) copy-start(bf16[4,6,24,512]{3,2,1,0:T(8,128)(2,1)} %param.8) | copy-start | bytes 1769476
Sparse Core Ops, SparseCore 0:
  62.9 52.4 reduce-scatter.8
  117.8 35.4 reduce-scatter.10
  157.0 67.5 reduce-scatter.12
  229.2 64.0 reduce-scatter.14
where the time goes:
time: 301 us; the launch traced here: 300 us
  waiting for transfers between devices  233 us (77%)
  Pallas kernels  20.7 us (7%)
  local copies, waits for them, and re-layouts  19.2 us (6%)
  between operations  14.1 us (5%)
  starting transfers between devices  9.47 us (3%)
  other arithmetic  3.8 us (1%)
    unnamed x6, waiting for transfers between devices  136 us
    reduce_scatter x1, waiting for transfers between devices, on_device(): lax.psum_scatter(grad_qkv, 'lat', scatter_dimension=0, tiled=True)  45.2 us
    reduce_scatter x1, waiting for transfers between devices, on_device(): lax.psum_scatter(grad_out, 'lat', scatter_dimension=0, tiled=True)  26.1 us
    ppermute x4, waiting for transfers between devices, from_behind(): lax.ppermute(array, axis, [(i, (i + by) % count) for i in range(count)])  25.3 us
    pallas_call x1, Pallas kernels, compute(): pl.pallas_call(compute_kernel, out_shape=(jax.ShapeDtypeStruct((tokens, w...  20.7 us
    unnamed x25, local copies, waits for them, and re-layouts  11.5 us
    ppermute x4, starting transfers between devices, from_behind(): lax.ppermute(array, axis, [(i, (i + by) % count) for i in range(count)])  9.14 us
  transfers between devices with their start and end apart: 8, of which 7 were waited for; matrix products, arithmetic and copies ran while one was open for 5% of the time, Pallas kernels for 0%

commit v1 on v0

v1 whole, which is shorter than its diff:
```python
import functools

import jax
import jax.numpy as jnp
import numpy as np
from jax import lax
from jax.experimental import pallas as pl
from jax.experimental.pallas import tpu as pltpu
from jax.sharding import PartitionSpec as P

SPAN = 144
TOKENS = 576
PACKED = 640
WIDTH = 512
NN = (((1,), (0,)), ((), ()))
NT = (((1,), (1,)), ((), ()))
BF = jnp.bfloat16
F32 = jnp.float32
MESH = pl.DeviceIdType.MESH

SECTIONS = (
    ("local", 0, 224, (0, 0)),
    ("lat+", 224, 112, (1, 0)),
    ("lat-", 336, 112, (-1, 0)),
    ("lon+", 448, 48, (0, 1)),
    ("lon-", 496, 48, (0, -1)),
    ("diag+", 544, 48, (1, 1)),
    ("diag-", 592, 48, (-1, -1)),
)
GOES = {
    (0, 0, 1): "local", (0, 1, 1): "lat+", (0, 0, 0): "local",
    (0, 0, 2): "lon+", (0, 1, 0): "lat+", (0, 1, 2): "diag+",
    (1, 1, 1): "local", (1, 0, 1): "lat-", (1, 1, 2): "local",
    (1, 1, 0): "lon-", (1, 0, 2): "lat-", (1, 0, 0): "diag-",
}
ORDERS = ((2, 1, 0), (1, 0, 2), (0, 2, 1), (0, 1, 2))


def constants():
    pack = np.zeros((PACKED, TOKENS), np.float32)
    window = np.zeros((TOKENS, PACKED), np.float32)
    first = {name: row for name, row, _, _ in SECTIONS}
    filled = dict.fromkeys(first, 0)
    for t in range(TOKENS):
        l, a, o = t // 144, t // 24 % 6, t % 24
        level = (l + 1) % 4
        piece = 0 if o < 6 else 1 if o < 18 else 2
        name = GOES[level // 2, a // 3, piece]
        row = first[name] + filled[name]
        filled[name] += 1
        pack[row, t] = 1
        column = (o + 6) % 12
        which = level // 2 * 2 + (0 if piece == 1 else 1)
        window[which * SPAN + level % 2 * 72 + (a + 3) % 6 * 12 + column, row] = 1
    row_of = np.zeros((TOKENS, 48), np.float32)
    column_of = np.zeros((TOKENS, 128), np.float32)
    for which in range(4):
        source = (0, 0, 1, 2)[which]
        for n in range(SPAN):
            t = which * SPAN + n
            row_of[t, (source * 2 + n // 72) * 8 + n // 12 % 6] = 1
            column_of[t, n % 12 + (12 if which % 2 == 0 else 0)] = 1
    mix = np.zeros((512, 512), np.float32)
    for jj in range(4):
        for r in range(96):
            mix[96 * jj + r, 128 * jj + r] = 1
        for r in range(32):
            mix[384 + 32 * jj + r, 128 * jj + 96 + r] = 1
    eye = np.eye(SPAN, dtype=np.float32)
    made = pack, window, pack.T, window.T, row_of, column_of, mix, eye
    return [jnp.asarray(m, BF) for m in made]


def dot(a, b, dims=NN):
    return lax.dot_general(a, b, dims, preferred_element_type=F32)


def kernel(x_hbm, cot_hbm, region_ref, gain_ref, w_hbm, wo_hbm,
           pack_hbm, window_hbm, unpack_hbm, unwindow_hbm, row_ref, column_ref, mix_hbm, eye_ref,
           result_ref, grad_ref, owned_ref,
           x_ref, cot_ref, w_ref, wo_ref, pack_ref, window_ref, unpack_ref, unwindow_ref, mix_ref,
           px_ref, pc_ref, rx_ref, rc_ref, regions_ref, rr_ref, hot_ref,
           xw_ref, cw_ref, normed_ref, nbf_ref, inv_ref, proj_ref, aw_ref, att_ref, ga_ref, gp_ref, tr_ref,
           po_ref, pg_ref, ro_ref, rg_ref,
           gb_ref, r0_ref, s0_ref, r1_ref, s1_ref, r2_ref, s2_ref, r3_ref,
           load_sem, halo_send, halo_recv, region_send, region_recv, rs_send, rs_recv):
    lat, lon = lax.axis_index("lat"), lax.axis_index("lon")
    core = lon % 2
    at = (lon // 8 * 2 + lat // 4, lon // 2 % 4, lat % 4)

    def near(step):
        return ((lat + step[0] + 8) % 8, (lon + step[1] + 16) % 16)

    def chip(x, y, z, c):
        return (x % 2 * 4 + z, (x // 2 * 4 + y) * 2 + c)

    def along(axis, k):
        there = list(at)
        there[axis] = (at[axis] + k) % 4
        return chip(*there, core)

    partners = [near(step) for _, _, _, step in SECTIONS[1:]]
    partners += [chip(*at, 1 - core)]
    partners += [along(axis, k) for axis in range(3) for k in (1, 2, 3)]
    barrier = pltpu.get_barrier_semaphore()
    for partner in partners:
        pl.semaphore_signal(barrier, inc=1, device_id=partner, device_id_type=MESH)

    loads = [
        pltpu.make_async_copy(src, dst, load_sem.at[n])
        for n, (src, dst) in enumerate((
            (pack_hbm, pack_ref), (x_hbm, x_ref), (cot_hbm, cot_ref), (window_hbm, window_ref), (w_hbm, w_ref),
            (wo_hbm, wo_ref), (unwindow_hbm, unwindow_ref), (mix_hbm, mix_ref), (unpack_hbm, unpack_ref),
        ))
    ]
    for load in loads:
        load.start()

    def halo(which, src, dst, back):
        made = []
        for n, (_, row, rows, step) in enumerate(SECTIONS[1:]):
            to = near((-step[0], -step[1])) if back else near(step)
            made.append(pltpu.make_async_remote_copy(
                src_ref=src.at[pl.ds(row, rows)], dst_ref=dst.at[pl.ds(row, rows)],
                send_sem=halo_send.at[which, n], recv_sem=halo_recv.at[which, n],
                device_id=to, device_id_type=MESH))
        return made

    loads[0].wait()
    loads[1].wait()
    px_ref[...] = dot(pack_ref[...], x_ref[...]).astype(BF)
    pl.semaphore_wait(barrier, len(partners))
    go_x = halo(0, px_ref, rx_ref, False)
    for copy in go_x:
        copy.start()
    go_regions = [
        pltpu.make_async_remote_copy(
            src_ref=region_ref.at[pl.ds(2, 2)], dst_ref=regions_ref.at[n],
            send_sem=region_send.at[n], recv_sem=region_recv.at[n],
            device_id=near(step), device_id_type=MESH)
        for n, step in enumerate(((-1, 0), (-1, -1)))
    ]
    for copy in go_regions:
        copy.start()
    loads[2].wait()
    pc_ref[...] = dot(pack_ref[...], cot_ref[...]).astype(BF)
    go_cot = halo(1, pc_ref, rc_ref, False)
    for copy in go_cot:
        copy.start()
    rx_ref[pl.ds(0, 224), :] = px_ref[pl.ds(0, 224), :]
    rc_ref[pl.ds(0, 224), :] = pc_ref[pl.ds(0, 224), :]

    for copy in go_regions:
        copy.wait_recv()
    rr_ref[...] = jnp.zeros_like(rr_ref)
    for n in range(6):
        piece = region_ref[n % 2] if n < 2 else regions_ref[n // 2 - 1, n % 2]
        rr_ref[pl.ds(8 * n, 6), pl.ds(0, 24)] = piece.astype(F32)
    picked = dot(row_ref[...], rr_ref[...].astype(BF)) * column_ref[...].astype(F32)
    value = dot(picked.astype(BF), jnp.ones((128, 128), BF))
    lanes = lax.broadcasted_iota(jnp.int32, (TOKENS, 128), 1).astype(F32)
    hot_ref[...] = jnp.where(value == lanes, 1.0, 0.0).astype(BF)

    gain = gain_ref[...]
    loads[3].wait()
    for copy in go_x:
        copy.wait_recv()
    for w in range(4):
        rows = pl.ds(w * SPAN, SPAN)
        x = dot(window_ref[rows, :], rx_ref[...])
        xw_ref[rows, :] = x.astype(BF)
        centered = x - jnp.mean(x, -1, keepdims=True)
        var = jnp.mean(centered * centered, -1, keepdims=True)
        inv = lax.rsqrt(var + 1e-5)
        normed = centered * inv
        normed_ref[rows, :] = normed
        inv_ref[rows, :] = inv
        nbf_ref[rows, :] = (normed * gain).astype(BF)
    loads[4].wait()
    for c in range(6):
        cols = pl.ds(c * 256, 256)
        proj_ref[:, cols] = dot(nbf_ref[...], w_ref[:, cols]).astype(BF)

    lane = lax.broadcasted_iota(jnp.int32, (1, 128), 1)
    masks = [jnp.where((lane < 64) == (h == 0), 1.0, 0.0).astype(BF) for h in range(2)]
    eighths = [(m * 0.125).astype(BF) for m in masks]

    def forward(p, _):
        col = pl.multiple_of(p * 128, 128)
        for w in range(4):
            rows = pl.ds(w * SPAN, SPAN)
            q2 = proj_ref[rows, pl.ds(col, 128)]
            k2 = proj_ref[rows, pl.ds(pl.multiple_of(512 + col, 128), 128)]
            v2 = proj_ref[rows, pl.ds(pl.multiple_of(1024 + col, 128), 128)]
            hot = hot_ref[rows, :]
            qx = jnp.concatenate([q2, hot * jnp.array(-1e30, BF)], 1)
            off = (1.0 - hot.astype(F32)).astype(BF)
            att = []
            for h in range(2):
                s = dot(qx, jnp.concatenate([k2 * eighths[h], off], 1), NT)
                e = jnp.exp(s - jnp.max(s, -1, keepdims=True))
                a = e * (1.0 / jnp.sum(e, -1, keepdims=True))
                aw_ref[p, w, h] = a
                att.append(dot(a.astype(BF), v2))
            att_ref[rows, pl.ds(col, 128)] = jnp.where(lane < 64, att[0], att[1]).astype(BF)
        return 0

    lax.fori_loop(0, 4, forward, 0)

    loads[5].wait()
    for w in range(4):
        rows = pl.ds(w * SPAN, SPAN)
        branch = dot(att_ref[rows, :], wo_ref[...])
        xw_ref[rows, :] = (xw_ref[rows, :].astype(F32) + branch).astype(BF)
    loads[6].wait()
    po_ref[...] = dot(unwindow_ref[...], xw_ref[...]).astype(BF)
    go_out = halo(2, po_ref, ro_ref, True)
    for copy in go_out:
        copy.start()
    ro_ref[pl.ds(0, 224), :] = po_ref[pl.ds(0, 224), :]

    for copy in go_cot:
        copy.wait_recv()
    cw_ref[...] = dot(window_ref[...], rc_ref[...]).astype(BF)
    for c in range(2):
        ga_ref[:, pl.ds(c * 256, 256)] = dot(cw_ref[...], wo_ref[pl.ds(c * 256, 256), :], NT).astype(BF)
    eye = eye_ref[...]
    eye128 = eye_ref[:128, :128]

    def backward(p, _):
        col = pl.multiple_of(p * 128, 128)
        for w in range(4):
            rows = pl.ds(w * SPAN, SPAN)
            q2 = proj_ref[rows, pl.ds(col, 128)]
            k2 = proj_ref[rows, pl.ds(pl.multiple_of(512 + col, 128), 128)]
            v2 = proj_ref[rows, pl.ds(pl.multiple_of(1024 + col, 128), 128)]
            g2 = ga_ref[rows, pl.ds(col, 128)]
            qt = dot(eye128, q2 * jnp.array(0.125, BF), NT).astype(BF)
            gt = dot(eye128, g2, NT).astype(BF)
            gq = None
            gkt = []
            gvt = []
            for h in range(2):
                a = aw_ref[p, w, h]
                gw = dot(g2, v2 * masks[h], NT)
                prod = gw * a
                inner = jnp.sum(prod, -1, keepdims=True)
                ds = (prod - a * inner).astype(BF)
                part = dot(ds, k2 * eighths[h])
                gq = part if gq is None else gq + part
                gkt.append(dot(qt[64 * h:64 * h + 64], ds))
                gvt.append(dot(gt[64 * h:64 * h + 64], a.astype(BF)))
            gk = dot(eye, jnp.concatenate(gkt, 0).astype(BF), NT)
            gv = dot(eye, jnp.concatenate(gvt, 0).astype(BF), NT)
            gp_ref[rows, pl.ds(col, 128)] = gq.astype(BF)
            gp_ref[rows, pl.ds(pl.multiple_of(512 + col, 128), 128)] = gk.astype(BF)
            gp_ref[rows, pl.ds(pl.multiple_of(1024 + col, 128), 128)] = gv.astype(BF)
        return 0

    lax.fori_loop(0, 4, backward, 0)

    tr_ref[0] = nbf_ref[...].T
    tr_ref[1] = att_ref[...].T
    loads[7].wait()
    for m in range(4):
        gm = dot(tr_ref[0], gp_ref[:, pl.ds(384 * m, 384)]).astype(BF)
        om = dot(tr_ref[1], cw_ref[:, pl.ds(128 * m, 128)]).astype(BF)
        mixed = dot(jnp.concatenate([gm, om], 1), mix_ref[...]).astype(BF)
        for jj in range(4):
            j = 4 * m + jj
            for i in range(8):
                gb_ref[j % 2, j // 8 * 2 + i // 4, j // 2 % 4, i % 4] = mixed[64 * i:64 * i + 64, 128 * jj:128 * jj + 128]

    def swap(n):
        return pltpu.make_async_remote_copy(
            src_ref=gb_ref.at[1 - core, n], dst_ref=r0_ref.at[n],
            send_sem=rs_send.at[n], recv_sem=rs_recv.at[n],
            device_id=chip(*at, 1 - core), device_id_type=MESH)

    swaps = [swap(n) for n in range(4)]
    for copy in swaps:
        copy.start()

    for w in range(4):
        rows = pl.ds(w * SPAN, SPAN)
        gh = dot(gp_ref[rows, :], w_ref[...], NT) * gain
        normed = normed_ref[rows, :]
        gs = inv_ref[rows, :] * (gh - jnp.mean(gh, -1, keepdims=True)
                                 - normed * jnp.mean(gh * normed, -1, keepdims=True))
        nbf_ref[rows, :] = gs.astype(BF)
    pg_ref[...] = dot(unwindow_ref[...], nbf_ref[...]).astype(BF)
    go_grad = halo(3, pg_ref, rg_ref, True)
    for copy in go_grad:
        copy.start()
    rg_ref[pl.ds(0, 224), :] = pg_ref[pl.ds(0, 224), :]

    for n in range(4):
        swaps[n].wait_recv()

        def add(y, _, n=n):
            s0_ref[n, y] = (gb_ref[core, n, y].astype(F32) + r0_ref[n, y].astype(F32)).astype(BF)
            return 0

        lax.fori_loop(0, 4, add, 0)

    def scatter(stage, s, k, src, dst):
        n = 4 + (stage * 4 + s) * 3 + k - 1
        return pltpu.make_async_remote_copy(
            src_ref=src, dst_ref=dst, send_sem=rs_send.at[n], recv_sem=rs_recv.at[n],
            device_id=along(ORDERS[s][stage], k), device_id_type=MESH)

    def quarter(s, axis, index):
        rows = pl.ds(16 * s, 16)
        if axis == 0:
            return s0_ref.at[index, :, :, rows]
        if axis == 1:
            return s0_ref.at[:, index, :, rows]
        return s0_ref.at[:, :, index, rows]

    sent = []
    first = [[scatter(0, s, k, quarter(s, ORDERS[s][0], (at[ORDERS[s][0]] + k) % 4), r1_ref.at[s, k - 1])
              for k in (1, 2, 3)] for s in range(4)]
    for k in range(3):
        for s in range(4):
            first[s][k].start()
    loads[8].wait()
    for copy in go_out:
        copy.wait_recv()
    result_ref[...] = dot(unpack_ref[...], ro_ref[...]).astype(BF)

    second = []
    for s in range(4):
        axis, nxt = ORDERS[s][0], ORDERS[s][1]
        for copy in first[s]:
            copy.wait_recv()
        total = quarter(s, axis, at[axis])[...].astype(F32)
        for k in range(3):
            total = total + r1_ref[s, k].astype(F32)
        s1_ref[s] = total
        copies = []
        for k in (1, 2, 3):
            there = (at[nxt] + k) % 4
            left = [a for a in range(3) if a != axis]
            src = s1_ref.at[s, there] if left[0] == nxt else s1_ref.at[s, :, there]
            copies.append(scatter(1, s, k, src, r2_ref.at[s, k - 1]))
            copies[-1].start()
        second.append(copies)
    third = []
    for s in range(4):
        axis, nxt, last = ORDERS[s]
        for copy in second[s]:
            copy.wait_recv()
        left = [a for a in range(3) if a != axis]
        total = s1_ref[s, at[nxt]] if left[0] == nxt else s1_ref[s, :, at[nxt]]
        for k in range(3):
            total = total + r2_ref[s, k]
        s2_ref[s] = total
        copies = []
        for k in (1, 2, 3):
            copies.append(scatter(2, s, k, s2_ref.at[s, (at[last] + k) % 4], r3_ref.at[s, k - 1]))
            copies[-1].start()
        third.append(copies)
    for copy in go_grad:
        copy.wait_recv()
    grad_ref[...] = (cot_ref[...].astype(F32) + dot(unpack_ref[...], rg_ref[...])).astype(BF)
    for s in range(4):
        for copy in third[s]:
            copy.wait_recv()
        total = s2_ref[s, at[ORDERS[s][2]]]
        for k in range(3):
            total = total + r3_ref[s, k]
        owned_ref[pl.ds(16 * s, 16), :] = total

    started = go_x + go_regions + go_cot + go_out + go_grad + swaps
    for copies in first + second + third:
        started += copies
    for copy in started:
        copy.wait_send()


def on_device(tokens, cotangent, region_ids, norm_gain, qkv_weight, out_weight):
    pack, window, unpack, unwindow, row_of, column_of, mix, eye = constants()
    vm = pl.BlockSpec(memory_space=pltpu.VMEM)
    hbm = pl.BlockSpec(memory_space=pl.ANY)

    def bf(*shape):
        return pltpu.VMEM(shape, BF)

    def f32(*shape):
        return pltpu.VMEM(shape, F32)

    result, grad, owned = pl.pallas_call(
        kernel,
        out_shape=(
            jax.ShapeDtypeStruct((TOKENS, WIDTH), BF),
            jax.ShapeDtypeStruct((TOKENS, WIDTH), BF),
            jax.ShapeDtypeStruct((64, 128), F32),
        ),
        in_specs=[hbm, hbm, vm, vm, hbm, hbm, hbm, hbm, hbm, hbm, vm, vm, hbm, vm],
        out_specs=(vm, vm, vm),
        scratch_shapes=[
            bf(TOKENS, WIDTH), bf(TOKENS, WIDTH), bf(WIDTH, 3 * WIDTH), bf(WIDTH, WIDTH),
            bf(PACKED, TOKENS), bf(TOKENS, PACKED), bf(TOKENS, PACKED), bf(PACKED, TOKENS), bf(512, 512),
            bf(PACKED, WIDTH), bf(PACKED, WIDTH), bf(PACKED, WIDTH), bf(PACKED, WIDTH),
            pltpu.VMEM((2, 2, 6, 24), jnp.int32), f32(48, 128), bf(TOKENS, 128),
            bf(TOKENS, WIDTH), bf(TOKENS, WIDTH), f32(TOKENS, WIDTH), bf(TOKENS, WIDTH), f32(TOKENS, 1),
            bf(TOKENS, 3 * WIDTH), f32(4, 4, 2, SPAN, SPAN), bf(TOKENS, WIDTH), bf(TOKENS, WIDTH),
            bf(TOKENS, 3 * WIDTH), bf(2, WIDTH, TOKENS),
            bf(PACKED, WIDTH), bf(PACKED, WIDTH), bf(PACKED, WIDTH), bf(PACKED, WIDTH),
            bf(2, 4, 4, 4, 64, 128), bf(4, 4, 4, 64, 128), bf(4, 4, 4, 64, 128),
            bf(4, 3, 4, 4, 16, 128), f32(4, 4, 4, 16, 128),
            f32(4, 3, 4, 16, 128), f32(4, 4, 16, 128), f32(4, 3, 16, 128),
            pltpu.SemaphoreType.DMA((9,)),
            pltpu.SemaphoreType.DMA((4, 6)), pltpu.SemaphoreType.DMA((4, 6)),
            pltpu.SemaphoreType.DMA((2,)), pltpu.SemaphoreType.DMA((2,)),
            pltpu.SemaphoreType.DMA((40,)), pltpu.SemaphoreType.DMA((40,)),
        ],
        compiler_params=pltpu.CompilerParams(
            vmem_limit_bytes=56 << 20, collective_id=0, has_side_effects=True),
        cost_estimate=pl.CostEstimate(flops=6 * 10**9, bytes_accessed=10**7, transcendentals=0),
    )(
        tokens.reshape(TOKENS, WIDTH), cotangent.reshape(TOKENS, WIDTH), region_ids, norm_gain.reshape(1, WIDTH),
        qkv_weight, out_weight, pack, window, unpack, unwindow, row_of, column_of, mix, eye,
    )
    return (result.reshape(tokens.shape), grad.reshape(tokens.shape), owned[:, :96], owned[:, 96:])


def solution(mesh):
    placed = (
        P(None, "lat", "lon", None),
        P(None, "lat", "lon", None),
        P(None, "lat", "lon"),
        P(),
        P(),
        P(),
    )
    return jax.shard_map(
        on_device,
        mesh=mesh,
        in_specs=placed,
        out_specs=(
            P(None, "lat", "lon", None),
            P(None, "lat", "lon", None),
            P("lat", "lon"),
            P("lat", "lon"),
        ),
        check_vma=False,
    )
```

time: 301 us -> 70.2 us (0.23)
  waiting for transfers between devices: 233 us -> 0 us
  Pallas kernels: 20.7 us -> 62.5 us
  between operations: 14.1 us -> 0.66 us
  local copies, waits for them, and re-layouts: 19.2 us -> 6.25 us
  starting transfers between devices: 9.47 us -> 0 us
  other arithmetic: 3.8 us -> 0 us
    unnamed x6 -> x0, waiting for transfers between devices: 136 us -> none
    reduce_scatter x2 -> x0, waiting for transfers between devices: 71.3 us -> none  [the longest x1 45.2 us: on_device(): lax.psum_scatter(grad_qkv, 'lat', scatter_dimension=0, tiled=True)]
    pallas_call x1, Pallas kernels: 20.7 us -> 62.5 us  [on_device(): pl.pallas_call(kernel, out_shape=(jax.ShapeDtypeStruct((TOKENS, WIDTH), B...]
    ppermute x4 -> x0, waiting for transfers between devices: 25.3 us -> none  [from_behind(): lax.ppermute(array, axis, [(i, (i + by) % count) for i in range(count)])]
    ppermute x4 -> x0, starting transfers between devices: 9.14 us -> none  [from_behind(): lax.ppermute(array, axis, [(i, (i + by) % count) for i in range(count)])]
    unnamed x25 -> x9, local copies, waits for them, and re-layouts: 11.5 us -> 5.36 us
  transfers between devices with their start and end apart: 8 -> 0, of which waited for: 7 -> 0; matrix products, arithmetic and copies ran while one was open for 5% -> 0% of each run, Pallas kernels for 0% -> 0%
where the time goes in v1:
time: 70.2 us; the launch traced here: 69.4 us
  Pallas kernels  62.5 us (89%)
  local copies, waits for them, and re-layouts  6.25 us (9%)
    pallas_call x1, Pallas kernels, on_device(): pl.pallas_call(kernel, out_shape=(jax.ShapeDtypeStruct((TOKENS, WIDTH), B...  62.5 us
    unnamed x9, local copies, waits for them, and re-layouts  5.36 us

profile of v1, /device:TPU:1, one launch (start us, length us, event | category | flops | bytes accessed | tf_op | source)
XLA Modules:
  0.0 69.4 jit_solution(15178776639278811691)
XLA Ops:
  0.6 1.3 %copy.18.region_ref = s32[4,6,24]{2,1,0:T(8,128)} copy(s32[4,6,24]{2,0,1:T(4,128)} %param.16) | data formatting | bytes 4608 | tf_op args[2]
  1.9 62.5 %shard_map.165 = (bf16[576,512]{1,0:T(8,128)(2,1)}, bf16[576,512]{1,0:T(8,128)(2,1)}, f32[64,128]{1,0:T(8,128)}) custom-call(bf16[576,512]{1,0:T(8,128)(2,1)} %bitcast.9, bf16[576,512]{1,0:T(8,128)(2,1)} %bitcast.10, s32[4,6,24]{2,1,0:T(8,128)} %copy.18.region_ref, f32[1,512]{1,0:T(1,128)} %bitcast.11, bf16[512,1536]{1,0:T(8,128)(2,1)} %w_hbm.1, ...), custom_call_target="tpu_custom_call" | custom-call | flops 6000000000 | bytes 10000000 | tf_op jit(solution)/shard_map/pallas_call | solution.py:392
  64.4 0.0 copy-start
  64.4 0.0 copy-start.1
  64.4 0.9 %slice.7 = f32[64,32]{1,0:T(8,128)S(1)} slice(f32[64,128]{1,0:T(8,128)} %get-tuple-element.9), slice={[0:64], [96:128]} | slice | bytes 16384 | tf_op jit(solution)/shard_map/slice | solution.py:425
  65.3 0.7 copy.19
  66.0 1.9 %copy.23 = bf16[4,6,24,512]{3,2,1,0:T(8,128)(2,1)} copy(bf16[4,6,24,512]{3,2,1,0:T(8,128)(2,1)} %bitcast.7) | data formatting | bytes 1179648
  67.9 0.0 copy-done
  67.9 0.8 %copy.24 = bf16[4,6,24,512]{3,2,1,0:T(8,128)(2,1)} copy(bf16[4,6,24,512]{3,2,1,0:T(8,128)(2,1)S(1)} %bitcast.6) | data formatting | bytes 1179648
  68.8 0.0 copy-done.1
  68.8 0.6 copy.25
Async XLA Ops:
  64.4 3.5 %copy-start = (bf16[576,512]{1,0:T(8,128)(2,1)S(1)}, bf16[576,512]{1,0:T(8,128)(2,1)}, u32[]{:S(2)}) copy-start(bf16[576,512]{1,0:T(8,128)(2,1)} %get-tuple-element.8) | copy-start | bytes 1769476
  64.4 4.3 %copy-start.1 = (f32[64,128]{1,0:T(8,128)S(1)}, f32[64,128]{1,0:T(8,128)}, u32[]{:S(2)}) copy-start(f32[64,128]{1,0:T(8,128)} %get-tuple-element.9) | copy-start | bytes 98308

commit v2 on v1

--- a/solution.py
+++ b/solution.py
@@ -52,22 +52,15 @@
         column = (o + 6) % 12
         which = level // 2 * 2 + (0 if piece == 1 else 1)
         window[which * SPAN + level % 2 * 72 + (a + 3) % 6 * 12 + column, row] = 1
-    row_of = np.zeros((TOKENS, 48), np.float32)
+    row_of = np.zeros((TOKENS, 144), np.float32)
     column_of = np.zeros((TOKENS, 128), np.float32)
     for which in range(4):
         source = (0, 0, 1, 2)[which]
         for n in range(SPAN):
             t = which * SPAN + n
-            row_of[t, (source * 2 + n // 72) * 8 + n // 12 % 6] = 1
+            row_of[t, (source * 6 + n // 12 % 6) * 8 + n // 72 + (2 if source else 0)] = 1
             column_of[t, n % 12 + (12 if which % 2 == 0 else 0)] = 1
-    mix = np.zeros((512, 512), np.float32)
-    for jj in range(4):
-        for r in range(96):
-            mix[96 * jj + r, 128 * jj + r] = 1
-        for r in range(32):
-            mix[384 + 32 * jj + r, 128 * jj + 96 + r] = 1
-    eye = np.eye(SPAN, dtype=np.float32)
-    made = pack, window, pack.T, window.T, row_of, column_of, mix, eye
+    made = pack, window, pack.T, window.T, row_of, column_of
     return [jnp.asarray(m, BF) for m in made]
 
 
@@ -76,13 +69,13 @@
 
 
 def kernel(x_hbm, cot_hbm, region_ref, gain_ref, w_hbm, wo_hbm,
-           pack_hbm, window_hbm, unpack_hbm, unwindow_hbm, row_ref, column_ref, mix_hbm, eye_ref,
-           result_ref, grad_ref, owned_ref,
-           x_ref, cot_ref, w_ref, wo_ref, pack_ref, window_ref, unpack_ref, unwindow_ref, mix_ref,
+           pack_hbm, window_hbm, unpack_hbm, unwindow_hbm, row_ref, column_ref,
+           result_ref, grad_ref, gq_ref, go_ref,
+           x_ref, cot_ref, w_ref, wo_ref, pack_ref, window_ref, unpack_ref, unwindow_ref,
            px_ref, pc_ref, rx_ref, rc_ref, regions_ref, rr_ref, hot_ref,
            xw_ref, cw_ref, normed_ref, nbf_ref, inv_ref, proj_ref, aw_ref, att_ref, ga_ref, gp_ref, tr_ref,
            po_ref, pg_ref, ro_ref, rg_ref,
-           gb_ref, r0_ref, s0_ref, r1_ref, s1_ref, r2_ref, s2_ref, r3_ref,
+           gw_ref, r0_ref, s0_ref, r1_ref, s1_ref, r2_ref, s2_ref, r3_ref, fin_ref, all_ref,
            load_sem, halo_send, halo_recv, region_send, region_recv, rs_send, rs_recv):
     lat, lon = lax.axis_index("lat"), lax.axis_index("lon")
     core = lon % 2
@@ -102,19 +95,19 @@
     partners = [near(step) for _, _, _, step in SECTIONS[1:]]
     partners += [chip(*at, 1 - core)]
     partners += [along(axis, k) for axis in range(3) for k in (1, 2, 3)]
-    barrier = pltpu.get_barrier_semaphore()
-    for partner in partners:
-        pl.semaphore_signal(barrier, inc=1, device_id=partner, device_id_type=MESH)
-
     loads = [
         pltpu.make_async_copy(src, dst, load_sem.at[n])
         for n, (src, dst) in enumerate((
             (pack_hbm, pack_ref), (x_hbm, x_ref), (cot_hbm, cot_ref), (window_hbm, window_ref), (w_hbm, w_ref),
-            (wo_hbm, wo_ref), (unwindow_hbm, unwindow_ref), (mix_hbm, mix_ref), (unpack_hbm, unpack_ref),
+            (wo_hbm, wo_ref), (unwindow_hbm, unwindow_ref), (unpack_hbm, unpack_ref),
         ))
     ]
     for load in loads:
         load.start()
+
+    barrier = pltpu.get_barrier_semaphore()
+    for partner in partners:
+        pl.semaphore_signal(barrier, inc=1, device_id=partner, device_id_type=MESH)
 
     def halo(which, src, dst, back):
         made = []
@@ -135,7 +128,7 @@
         copy.start()
     go_regions = [
         pltpu.make_async_remote_copy(
-            src_ref=region_ref.at[pl.ds(2, 2)], dst_ref=regions_ref.at[n],
+            src_ref=region_ref, dst_ref=regions_ref.at[n],
             send_sem=region_send.at[n], recv_sem=region_recv.at[n],
             device_id=near(step), device_id_type=MESH)
         for n, step in enumerate(((-1, 0), (-1, -1)))
@@ -153,9 +146,9 @@
     for copy in go_regions:
         copy.wait_recv()
     rr_ref[...] = jnp.zeros_like(rr_ref)
-    for n in range(6):
-        piece = region_ref[n % 2] if n < 2 else regions_ref[n // 2 - 1, n % 2]
-        rr_ref[pl.ds(8 * n, 6), pl.ds(0, 24)] = piece.astype(F32)
+    for n in range(18):
+        piece = region_ref[n % 6] if n < 6 else regions_ref[n // 6 - 1, n % 6]
+        rr_ref[pl.ds(8 * n, 4), pl.ds(0, 24)] = piece.astype(F32)
     picked = dot(row_ref[...], rr_ref[...].astype(BF)) * column_ref[...].astype(F32)
     value = dot(picked.astype(BF), jnp.ones((128, 128), BF))
     lanes = lax.broadcasted_iota(jnp.int32, (TOKENS, 128), 1).astype(F32)
@@ -185,13 +178,13 @@
     masks = [jnp.where((lane < 64) == (h == 0), 1.0, 0.0).astype(BF) for h in range(2)]
     eighths = [(m * 0.125).astype(BF) for m in masks]
 
-    def forward(p, _):
-        col = pl.multiple_of(p * 128, 128)
+    def forward(p):
+        col = p * 128
         for w in range(4):
             rows = pl.ds(w * SPAN, SPAN)
             q2 = proj_ref[rows, pl.ds(col, 128)]
-            k2 = proj_ref[rows, pl.ds(pl.multiple_of(512 + col, 128), 128)]
-            v2 = proj_ref[rows, pl.ds(pl.multiple_of(1024 + col, 128), 128)]
+            k2 = proj_ref[rows, pl.ds(512 + col, 128)]
+            v2 = proj_ref[rows, pl.ds(1024 + col, 128)]
             hot = hot_ref[rows, :]
             qx = jnp.concatenate([q2, hot * jnp.array(-1e30, BF)], 1)
             off = (1.0 - hot.astype(F32)).astype(BF)
@@ -203,9 +196,9 @@
                 aw_ref[p, w, h] = a
                 att.append(dot(a.astype(BF), v2))
             att_ref[rows, pl.ds(col, 128)] = jnp.where(lane < 64, att[0], att[1]).astype(BF)
-        return 0
-
-    lax.fori_loop(0, 4, forward, 0)
+
+    for p in range(4):
+        forward(p)
 
     loads[5].wait()
     for w in range(4):
@@ -224,19 +217,16 @@
     cw_ref[...] = dot(window_ref[...], rc_ref[...]).astype(BF)
     for c in range(2):
         ga_ref[:, pl.ds(c * 256, 256)] = dot(cw_ref[...], wo_ref[pl.ds(c * 256, 256), :], NT).astype(BF)
-    eye = eye_ref[...]
-    eye128 = eye_ref[:128, :128]
-
-    def backward(p, _):
-        col = pl.multiple_of(p * 128, 128)
+    def backward(p):
+        col = p * 128
         for w in range(4):
             rows = pl.ds(w * SPAN, SPAN)
             q2 = proj_ref[rows, pl.ds(col, 128)]
-            k2 = proj_ref[rows, pl.ds(pl.multiple_of(512 + col, 128), 128)]
-            v2 = proj_ref[rows, pl.ds(pl.multiple_of(1024 + col, 128), 128)]
+            k2 = proj_ref[rows, pl.ds(512 + col, 128)]
+            v2 = proj_ref[rows, pl.ds(1024 + col, 128)]
             g2 = ga_ref[rows, pl.ds(col, 128)]
-            qt = dot(eye128, q2 * jnp.array(0.125, BF), NT).astype(BF)
-            gt = dot(eye128, g2, NT).astype(BF)
+            qt = (q2 * jnp.array(0.125, BF)).T
+            gt = g2.T
             gq = None
             gkt = []
             gvt = []
@@ -250,36 +240,31 @@
                 gq = part if gq is None else gq + part
                 gkt.append(dot(qt[64 * h:64 * h + 64], ds))
                 gvt.append(dot(gt[64 * h:64 * h + 64], a.astype(BF)))
-            gk = dot(eye, jnp.concatenate(gkt, 0).astype(BF), NT)
-            gv = dot(eye, jnp.concatenate(gvt, 0).astype(BF), NT)
             gp_ref[rows, pl.ds(col, 128)] = gq.astype(BF)
-            gp_ref[rows, pl.ds(pl.multiple_of(512 + col, 128), 128)] = gk.astype(BF)
-            gp_ref[rows, pl.ds(pl.multiple_of(1024 + col, 128), 128)] = gv.astype(BF)
-        return 0
-
-    lax.fori_loop(0, 4, backward, 0)
+            gp_ref[rows, pl.ds(512 + col, 128)] = jnp.concatenate(gkt, 0).astype(BF).T
+            gp_ref[rows, pl.ds(1024 + col, 128)] = jnp.concatenate(gvt, 0).astype(BF).T
+
+    def swap(first, count):
+        return pltpu.make_async_remote_copy(
+            src_ref=gw_ref.at[pl.ds(first, count), :, 1 - core], dst_ref=r0_ref.at[pl.ds(first, count)],
+            send_sem=rs_send.at[first], recv_sem=rs_recv.at[first],
+            device_id=chip(*at, 1 - core), device_id_type=MESH)
 
     tr_ref[0] = nbf_ref[...].T
     tr_ref[1] = att_ref[...].T
-    loads[7].wait()
     for m in range(4):
-        gm = dot(tr_ref[0], gp_ref[:, pl.ds(384 * m, 384)]).astype(BF)
-        om = dot(tr_ref[1], cw_ref[:, pl.ds(128 * m, 128)]).astype(BF)
-        mixed = dot(jnp.concatenate([gm, om], 1), mix_ref[...]).astype(BF)
-        for jj in range(4):
-            j = 4 * m + jj
-            for i in range(8):
-                gb_ref[j % 2, j // 8 * 2 + i // 4, j // 2 % 4, i % 4] = mixed[64 * i:64 * i + 64, 128 * jj:128 * jj + 128]
-
-    def swap(n):
-        return pltpu.make_async_remote_copy(
-            src_ref=gb_ref.at[1 - core, n], dst_ref=r0_ref.at[n],
-            send_sem=rs_send.at[n], recv_sem=rs_recv.at[n],
-            device_id=chip(*at, 1 - core), device_id_type=MESH)
-
-    swaps = [swap(n) for n in range(4)]
-    for copy in swaps:
-        copy.start()
+        block = pltpu.roll(dot(tr_ref[1], cw_ref[:, pl.ds(128 * m, 128)]), 64, 1)
+        gw_ref[12 + m] = block.reshape(8, 2, 32, 128)
+    swaps = [swap(12, 4)]
+    swaps[0].start()
+    for p in range(4):
+        backward(p)
+        pieces = jnp.concatenate([gp_ref[:, pl.ds(512 * t + 128 * p, 128)] for t in range(3)], 1)
+        grads = dot(tr_ref[0], pieces)
+        for t in range(3):
+            gw_ref[4 * t + p] = grads[:, 128 * t:128 * t + 128].reshape(8, 2, 32, 128)
+            swaps.append(swap(4 * t + p, 1))
+            swaps[-1].start()
 
     for w in range(4):
         rows = pl.ds(w * SPAN, SPAN)
@@ -288,42 +273,43 @@
         gs = inv_ref[rows, :] * (gh - jnp.mean(gh, -1, keepdims=True)
                                  - normed * jnp.mean(gh * normed, -1, keepdims=True))
         nbf_ref[rows, :] = gs.astype(BF)
-    pg_ref[...] = dot(unwindow_ref[...], nbf_ref[...]).astype(BF)
-    go_grad = halo(3, pg_ref, rg_ref, True)
-    for copy in go_grad:
-        copy.start()
-    rg_ref[pl.ds(0, 224), :] = pg_ref[pl.ds(0, 224), :]
-
-    for n in range(4):
-        swaps[n].wait_recv()
-
-        def add(y, _, n=n):
-            s0_ref[n, y] = (gb_ref[core, n, y].astype(F32) + r0_ref[n, y].astype(F32)).astype(BF)
-            return 0
-
-        lax.fori_loop(0, 4, add, 0)
+    for copy in swaps:
+        copy.wait_recv()
+    for m in range(4):
+        whole = [gw_ref[b, :, core] + r0_ref[b] for b in (3 * m, 3 * m + 1, 3 * m + 2, 12 + m)]
+        left = lane < 64
+        for n, parts in ((0, (whole[0], jnp.where(left, whole[1], whole[3]))),
+                         (1, (whole[2], jnp.where(left, whole[3], whole[1])))):
+            for half in range(2):
+                for x_lo in range(2):
+                    s0_ref[m // 2 * 2 + x_lo, m % 2 * 2 + n, :, half] = parts[half][4 * x_lo:4 * x_lo + 4].astype(BF)
 
     def scatter(stage, s, k, src, dst):
-        n = 4 + (stage * 4 + s) * 3 + k - 1
+        n = 16 + (stage * 4 + s) * 3 + k - 1
         return pltpu.make_async_remote_copy(
             src_ref=src, dst_ref=dst, send_sem=rs_send.at[n], recv_sem=rs_recv.at[n],
             device_id=along(ORDERS[s][stage], k), device_id_type=MESH)
 
     def quarter(s, axis, index):
-        rows = pl.ds(16 * s, 16)
+        half, rows = s // 2, pl.ds(s % 2 * 16, 16)
         if axis == 0:
-            return s0_ref.at[index, :, :, rows]
+            return s0_ref.at[index, :, :, half, rows]
         if axis == 1:
-            return s0_ref.at[:, index, :, rows]
-        return s0_ref.at[:, :, index, rows]
-
-    sent = []
+            return s0_ref.at[:, index, :, half, rows]
+        return s0_ref.at[:, :, index, half, rows]
+
     first = [[scatter(0, s, k, quarter(s, ORDERS[s][0], (at[ORDERS[s][0]] + k) % 4), r1_ref.at[s, k - 1])
               for k in (1, 2, 3)] for s in range(4)]
     for k in range(3):
         for s in range(4):
             first[s][k].start()
-    loads[8].wait()
+    pg_ref[...] = dot(unwindow_ref[...], nbf_ref[...]).astype(BF)
+    go_grad = halo(3, pg_ref, rg_ref, True)
+    for copy in go_grad:
+        copy.start()
+    rg_ref[pl.ds(0, 224), :] = pg_ref[pl.ds(0, 224), :]
+
+    loads[7].wait()
     for copy in go_out:
         copy.wait_recv()
     result_ref[...] = dot(unpack_ref[...], ro_ref[...]).astype(BF)
@@ -369,17 +355,36 @@
         total = s2_ref[s, at[ORDERS[s][2]]]
         for k in range(3):
             total = total + r3_ref[s, k]
-        owned_ref[pl.ds(16 * s, 16), :] = total
-
-    started = go_x + go_regions + go_cot + go_out + go_grad + swaps
+        fin_ref[pl.ds(s % 2 * 16, 16), pl.ds(s // 2 * 128, 128)] = total
+    last = pltpu.make_async_remote_copy(
+        src_ref=fin_ref, dst_ref=all_ref.at[core], send_sem=rs_send.at[52], recv_sem=rs_recv.at[52],
+        device_id=chip(*at, 1 - core), device_id_type=MESH)
+    last.start()
+    all_ref[core] = fin_ref[...]
+    last.wait_recv()
+    whole = all_ref[...].reshape(64, 256)
+    whole = jnp.where(at[1] % 2 == 1, pltpu.roll(whole, 64, 1), whole)
+    gq_ref[...] = jnp.where(core == 1, pltpu.roll(whole, 160, 1), whole)[:, :96]
+    outs = whole[:, 128:]
+    go_ref[...] = jnp.where(core == 1, pltpu.roll(outs, 32, 1), pltpu.roll(outs, 64, 1)).T[:32]
+
+    started = go_x + go_regions + go_cot + go_out + go_grad + swaps + [last]
     for copies in first + second + third:
         started += copies
     for copy in started:
         copy.wait_send()
 
 
+def hand_over(*refs):
+    copies = [pltpu.make_async_copy(refs[n], refs[4 + n], refs[8].at[n]) for n in range(4)]
+    for copy in copies:
+        copy.start()
+    for copy in copies:
+        copy.wait()
+
+
 def on_device(tokens, cotangent, region_ids, norm_gain, qkv_weight, out_weight):
-    pack, window, unpack, unwindow, row_of, column_of, mix, eye = constants()
+    pack, window, unpack, unwindow, row_of, column_of = constants()
     vm = pl.BlockSpec(memory_space=pltpu.VMEM)
     hbm = pl.BlockSpec(memory_space=pl.ANY)
 
@@ -389,40 +394,48 @@
     def f32(*shape):
         return pltpu.VMEM(shape, F32)
 
-    result, grad, owned = pl.pallas_call(
+    sums = pl.pallas_call(
         kernel,
         out_shape=(
             jax.ShapeDtypeStruct((TOKENS, WIDTH), BF),
             jax.ShapeDtypeStruct((TOKENS, WIDTH), BF),
-            jax.ShapeDtypeStruct((64, 128), F32),
+            jax.ShapeDtypeStruct((64, 96), F32),
+            jax.ShapeDtypeStruct((32, 64), F32),
         ),
-        in_specs=[hbm, hbm, vm, vm, hbm, hbm, hbm, hbm, hbm, hbm, vm, vm, hbm, vm],
-        out_specs=(vm, vm, vm),
+        in_specs=[hbm, hbm, vm, vm, hbm, hbm, hbm, hbm, hbm, hbm, vm, vm],
+        out_specs=(vm, vm, vm, vm),
         scratch_shapes=[
             bf(TOKENS, WIDTH), bf(TOKENS, WIDTH), bf(WIDTH, 3 * WIDTH), bf(WIDTH, WIDTH),
-            bf(PACKED, TOKENS), bf(TOKENS, PACKED), bf(TOKENS, PACKED), bf(PACKED, TOKENS), bf(512, 512),
+            bf(PACKED, TOKENS), bf(TOKENS, PACKED), bf(TOKENS, PACKED), bf(PACKED, TOKENS),
             bf(PACKED, WIDTH), bf(PACKED, WIDTH), bf(PACKED, WIDTH), bf(PACKED, WIDTH),
-            pltpu.VMEM((2, 2, 6, 24), jnp.int32), f32(48, 128), bf(TOKENS, 128),
+            pltpu.VMEM((2, 6, 4, 24), jnp.int32), f32(144, 128), bf(TOKENS, 128),
             bf(TOKENS, WIDTH), bf(TOKENS, WIDTH), f32(TOKENS, WIDTH), bf(TOKENS, WIDTH), f32(TOKENS, 1),
             bf(TOKENS, 3 * WIDTH), f32(4, 4, 2, SPAN, SPAN), bf(TOKENS, WIDTH), bf(TOKENS, WIDTH),
             bf(TOKENS, 3 * WIDTH), bf(2, WIDTH, TOKENS),
             bf(PACKED, WIDTH), bf(PACKED, WIDTH), bf(PACKED, WIDTH), bf(PACKED, WIDTH),
-            bf(2, 4, 4, 4, 64, 128), bf(4, 4, 4, 64, 128), bf(4, 4, 4, 64, 128),
+            f32(16, 8, 2, 32, 128), f32(16, 8, 32, 128), bf(4, 4, 4, 2, 32, 128),
             bf(4, 3, 4, 4, 16, 128), f32(4, 4, 4, 16, 128),
-            f32(4, 3, 4, 16, 128), f32(4, 4, 16, 128), f32(4, 3, 16, 128),
-            pltpu.SemaphoreType.DMA((9,)),
+            f32(4, 3, 4, 16, 128), f32(4, 4, 16, 128), f32(4, 3, 16, 128), f32(32, 256), f32(2, 32, 256),
+            pltpu.SemaphoreType.DMA((8,)),
             pltpu.SemaphoreType.DMA((4, 6)), pltpu.SemaphoreType.DMA((4, 6)),
             pltpu.SemaphoreType.DMA((2,)), pltpu.SemaphoreType.DMA((2,)),
-            pltpu.SemaphoreType.DMA((40,)), pltpu.SemaphoreType.DMA((40,)),
+            pltpu.SemaphoreType.DMA((53,)), pltpu.SemaphoreType.DMA((53,)),
         ],
         compiler_params=pltpu.CompilerParams(
             vmem_limit_bytes=56 << 20, collective_id=0, has_side_effects=True),
         cost_estimate=pl.CostEstimate(flops=6 * 10**9, bytes_accessed=10**7, transcendentals=0),
     )(
-        tokens.reshape(TOKENS, WIDTH), cotangent.reshape(TOKENS, WIDTH), region_ids, norm_gain.reshape(1, WIDTH),
-        qkv_weight, out_weight, pack, window, unpack, unwindow, row_of, column_of, mix, eye,
+        tokens.reshape(TOKENS, WIDTH), cotangent.reshape(TOKENS, WIDTH), region_ids.transpose(1, 0, 2), norm_gain.reshape(1, WIDTH),
+        qkv_weight, out_weight, pack, window, unpack, unwindow, row_of, column_of,
     )
-    return (result.reshape(tokens.shape), grad.reshape(tokens.shape), owned[:, :96], owned[:, 96:])
+    result, grad, gq, go = pl.pallas_call(
+        hand_over,
+        out_shape=tuple(jax.ShapeDtypeStruct(a.shape, a.dtype) for a in sums),
+        in_specs=[hbm] * 4,
+        out_specs=(hbm,) * 4,
+        scratch_shapes=[pltpu.SemaphoreType.DMA((4,))],
+    )(*sums)
+    return (result.reshape(tokens.shape), grad.reshape(tokens.shape), gq, go.T)
 
 
 def solution(mesh):

time: 70.2 us -> 97.1 us (1.38)
  Pallas kernels: 62.5 us -> 96.1 us
  local copies, waits for them, and re-layouts: 6.25 us -> 0 us
    pallas_call x0 -> x1, Pallas kernels: none -> 38.4 us  [on_device(): pl.pallas_call(hand_over, out_shape=tuple((jax.ShapeDtypeStruct(a.shape,...]
    unnamed x9 -> x0, local copies, waits for them, and re-layouts: 5.36 us -> none
    pallas_call x1, Pallas kernels: 62.5 us -> 57.8 us  [on_device(): pl.pallas_call(kernel, out_shape=(jax.ShapeDtypeStruct((TOKENS, WIDTH), B...]
where the time goes in v2:
time: 97.1 us; the launch traced here: 96.9 us
  Pallas kernels  96.1 us (99%)
    pallas_call x1, Pallas kernels, on_device(): pl.pallas_call(kernel, out_shape=(jax.ShapeDtypeStruct((TOKENS, WIDTH), B...  57.8 us
    pallas_call x1, Pallas kernels, on_device(): pl.pallas_call(hand_over, out_shape=tuple((jax.ShapeDtypeStruct(a.shape,...  38.4 us

profile of v2, /device:TPU:1, one launch (start us, length us, event | category | flops | bytes accessed | tf_op | source)
XLA Modules:
  0.0 96.9 jit_solution(16052632900886696269)
XLA Ops:
  0.6 57.8 %shard_map.147 = (bf16[576,512]{1,0:T(8,128)(2,1)}, bf16[576,512]{1,0:T(8,128)(2,1)}, f32[64,96]{1,0:T(8,128)}, f32[32,64]{1,0:T(8,128)}) custom-call(bf16[576,512]{1,0:T(8,128)(2,1)} %bitcast.7, bf16[576,512]{1,0:T(8,128)(2,1)} %bitcast.8, s32[6,4,24]{2,1,0:T(4,128)} %bitcast.12, f32[1,512]{1,0:T(1,128)} %bitcast.13, bf16[512,1536]{1,0:T(8,128)(2,1)} %w_hbm.1, ...), custom_call_target="tpu_custom_call" | custom-call | flops 6000000000 | bytes 10000000 | tf_op jit(solution)/shard_map/pallas_call | solution.py:397
  58.4 38.4 %shard_map.148 = (bf16[576,512]{1,0:T(8,128)(2,1)}, bf16[576,512]{1,0:T(8,128)(2,1)}, f32[64,96]{1,0:T(8,128)}, f32[32,64]{1,0:T(8,128)}) custom-call(bf16[576,512]{1,0:T(8,128)(2,1)} %get-tuple-element.12.refs_0_, bf16[576,512]{1,0:T(8,128)(2,1)} %get-tuple-element.13.refs_1_, f32[64,96]{1,0:T(8,128)} %get-tuple-element.14.refs_2_, ...), custom_call_target="tpu_custom_call" | custom-call | tf_op jit(solution)/shard_map/pallas_call | solution.py:431

commit v3 on v2

--- a/solution.py
+++ b/solution.py
@@ -201,17 +201,6 @@
         forward(p)
 
     loads[5].wait()
-    for w in range(4):
-        rows = pl.ds(w * SPAN, SPAN)
-        branch = dot(att_ref[rows, :], wo_ref[...])
-        xw_ref[rows, :] = (xw_ref[rows, :].astype(F32) + branch).astype(BF)
-    loads[6].wait()
-    po_ref[...] = dot(unwindow_ref[...], xw_ref[...]).astype(BF)
-    go_out = halo(2, po_ref, ro_ref, True)
-    for copy in go_out:
-        copy.start()
-    ro_ref[pl.ds(0, 224), :] = po_ref[pl.ds(0, 224), :]
-
     for copy in go_cot:
         copy.wait_recv()
     cw_ref[...] = dot(window_ref[...], rc_ref[...]).astype(BF)
@@ -268,11 +257,8 @@
 
     for w in range(4):
         rows = pl.ds(w * SPAN, SPAN)
-        gh = dot(gp_ref[rows, :], w_ref[...], NT) * gain
-        normed = normed_ref[rows, :]
-        gs = inv_ref[rows, :] * (gh - jnp.mean(gh, -1, keepdims=True)
-                                 - normed * jnp.mean(gh * normed, -1, keepdims=True))
-        nbf_ref[rows, :] = gs.astype(BF)
+        branch = dot(att_ref[rows, :], wo_ref[...])
+        xw_ref[rows, :] = (xw_ref[rows, :].astype(F32) + branch).astype(BF)
     for copy in swaps:
         copy.wait_recv()
     for m in range(4):
@@ -303,16 +289,24 @@
     for k in range(3):
         for s in range(4):
             first[s][k].start()
+    loads[6].wait()
+    po_ref[...] = dot(unwindow_ref[...], xw_ref[...]).astype(BF)
+    go_out = halo(2, po_ref, ro_ref, True)
+    for copy in go_out:
+        copy.start()
+    ro_ref[pl.ds(0, 224), :] = po_ref[pl.ds(0, 224), :]
+    for w in range(4):
+        rows = pl.ds(w * SPAN, SPAN)
+        gh = dot(gp_ref[rows, :], w_ref[...], NT) * gain
+        normed = normed_ref[rows, :]
+        gs = inv_ref[rows, :] * (gh - jnp.mean(gh, -1, keepdims=True)
+                                 - normed * jnp.mean(gh * normed, -1, keepdims=True))
+        nbf_ref[rows, :] = gs.astype(BF)
     pg_ref[...] = dot(unwindow_ref[...], nbf_ref[...]).astype(BF)
     go_grad = halo(3, pg_ref, rg_ref, True)
     for copy in go_grad:
         copy.start()
     rg_ref[pl.ds(0, 224), :] = pg_ref[pl.ds(0, 224), :]
-
-    loads[7].wait()
-    for copy in go_out:
-        copy.wait_recv()
-    result_ref[...] = dot(unpack_ref[...], ro_ref[...]).astype(BF)
 
     second = []
     for s in range(4):
@@ -331,6 +325,11 @@
             copies.append(scatter(1, s, k, src, r2_ref.at[s, k - 1]))
             copies[-1].start()
         second.append(copies)
+    loads[7].wait()
+    for copy in go_out:
+        copy.wait_recv()
+    result_ref[...] = dot(unpack_ref[...], ro_ref[...]).astype(BF)
+
     third = []
     for s in range(4):
         axis, nxt, last = ORDERS[s]
@@ -376,11 +375,8 @@
 
 
 def hand_over(*refs):
-    copies = [pltpu.make_async_copy(refs[n], refs[4 + n], refs[8].at[n]) for n in range(4)]
-    for copy in copies:
-        copy.start()
-    for copy in copies:
-        copy.wait()
+    for n in range(4):
+        refs[4 + n][...] = refs[n][...]
 
 
 def on_device(tokens, cotangent, region_ids, norm_gain, qkv_weight, out_weight):
@@ -431,9 +427,8 @@
     result, grad, gq, go = pl.pallas_call(
         hand_over,
         out_shape=tuple(jax.ShapeDtypeStruct(a.shape, a.dtype) for a in sums),
-        in_specs=[hbm] * 4,
-        out_specs=(hbm,) * 4,
-        scratch_shapes=[pltpu.SemaphoreType.DMA((4,))],
+        in_specs=[vm] * 4,
+        out_specs=(vm,) * 4,
     )(*sums)
     return (result.reshape(tokens.shape), grad.reshape(tokens.shape), gq, go.T)
 

time: 97.1 us -> 63.8 us (0.66)
  Pallas kernels: 96.1 us -> 63 us
    pallas_call x1, Pallas kernels: 38.4 us -> 2.3 us  [on_device(): pl.pallas_call(hand_over, out_shape=tuple((jax.ShapeDtypeStruct(a.shape,...]
    pallas_call x1, Pallas kernels: 57.8 us -> 60.7 us  [on_device(): pl.pallas_call(kernel, out_shape=(jax.ShapeDtypeStruct((TOKENS, WIDTH), B...]
where the time goes in v3:
time: 63.8 us; the launch traced here: 63.7 us
  Pallas kernels  63 us (99%)
  between operations  0.64 us (1%)
    pallas_call x1, Pallas kernels, on_device(): pl.pallas_call(kernel, out_shape=(jax.ShapeDtypeStruct((TOKENS, WIDTH), B...  60.7 us
    pallas_call x1, Pallas kernels, on_device(): pl.pallas_call(hand_over, out_shape=tuple((jax.ShapeDtypeStruct(a.shape,...  2.3 us

profile of v3, /device:TPU:1, one launch (start us, length us, event | category | flops | bytes accessed | tf_op | source)
XLA Modules:
  0.0 63.7 jit_solution(5220301113226797610)
XLA Ops:
  0.6 60.7 %shard_map.147 = (bf16[576,512]{1,0:T(8,128)(2,1)}, bf16[576,512]{1,0:T(8,128)(2,1)}, f32[64,96]{1,0:T(8,128)}, f32[32,64]{1,0:T(8,128)}) custom-call(bf16[576,512]{1,0:T(8,128)(2,1)} %bitcast.7, bf16[576,512]{1,0:T(8,128)(2,1)} %bitcast.8, s32[6,4,24]{2,1,0:T(4,128)} %bitcast.12, f32[1,512]{1,0:T(1,128)} %bitcast.13, bf16[512,1536]{1,0:T(8,128)(2,1)} %w_hbm.1, ...), custom_call_target="tpu_custom_call" | custom-call | flops 6000000000 | bytes 10000000 | tf_op jit(solution)/shard_map/pallas_call | solution.py:393
  61.4 2.3 %shard_map.148 = (bf16[576,512]{1,0:T(8,128)(2,1)}, bf16[576,512]{1,0:T(8,128)(2,1)}, f32[64,96]{1,0:T(8,128)}, f32[32,64]{1,0:T(8,128)}) custom-call(bf16[576,512]{1,0:T(8,128)(2,1)} %get-tuple-element.12.refs_0_, bf16[576,512]{1,0:T(8,128)(2,1)} %get-tuple-element.13.refs_1_, f32[64,96]{1,0:T(8,128)} %get-tuple-element.14.refs_2_, ...), custom_call_target="tpu_custom_call" | custom-call | tf_op jit(solution)/shard_map/pallas_call | solution.py:427

commit v4 on v2

--- a/solution.py
+++ b/solution.py
@@ -33,8 +33,6 @@
     (1, 1, 1): "local", (1, 0, 1): "lat-", (1, 1, 2): "local",
     (1, 1, 0): "lon-", (1, 0, 2): "lat-", (1, 0, 0): "diag-",
 }
-ORDERS = ((2, 1, 0), (1, 0, 2), (0, 2, 1), (0, 1, 2))
-
 
 def constants():
     pack = np.zeros((PACKED, TOKENS), np.float32)
@@ -75,7 +73,7 @@
            px_ref, pc_ref, rx_ref, rc_ref, regions_ref, rr_ref, hot_ref,
            xw_ref, cw_ref, normed_ref, nbf_ref, inv_ref, proj_ref, aw_ref, att_ref, ga_ref, gp_ref, tr_ref,
            po_ref, pg_ref, ro_ref, rg_ref,
-           gw_ref, r0_ref, s0_ref, r1_ref, s1_ref, r2_ref, s2_ref, r3_ref, fin_ref, all_ref,
+           gw_ref, r0_ref, zs_ref, zr_ref, ps_ref, pr_ref, fin_ref, all_ref,
            load_sem, halo_send, halo_recv, region_send, region_recv, rs_send, rs_recv):
     lat, lon = lax.axis_index("lat"), lax.axis_index("lon")
     core = lon % 2
@@ -87,14 +85,14 @@
     def chip(x, y, z, c):
         return (x % 2 * 4 + z, (x // 2 * 4 + y) * 2 + c)
 
-    def along(axis, k):
-        there = list(at)
-        there[axis] = (at[axis] + k) % 4
-        return chip(*there, core)
-
+    def ahead(dx, dy, dz):
+        return chip((at[0] + dx) % 4, (at[1] + dy) % 4, (at[2] + dz) % 4, core)
+
+    steps = [(dx, dy) for dx in range(4) for dy in range(4) if dx or dy]
     partners = [near(step) for _, _, _, step in SECTIONS[1:]]
     partners += [chip(*at, 1 - core)]
-    partners += [along(axis, k) for axis in range(3) for k in (1, 2, 3)]
+    partners += [ahead(0, 0, k) for k in (1, 2, 3)]
+    partners += [ahead(dx, dy, 0) for dx, dy in steps]
     loads = [
         pltpu.make_async_copy(src, dst, load_sem.at[n])
         for n, (src, dst) in enumerate((
@@ -217,6 +215,7 @@
     cw_ref[...] = dot(window_ref[...], rc_ref[...]).astype(BF)
     for c in range(2):
         ga_ref[:, pl.ds(c * 256, 256)] = dot(cw_ref[...], wo_ref[pl.ds(c * 256, 256), :], NT).astype(BF)
+
     def backward(p):
         col = p * 128
         for w in range(4):
@@ -243,144 +242,134 @@
             gp_ref[rows, pl.ds(col, 128)] = gq.astype(BF)
             gp_ref[rows, pl.ds(512 + col, 128)] = jnp.concatenate(gkt, 0).astype(BF).T
             gp_ref[rows, pl.ds(1024 + col, 128)] = jnp.concatenate(gvt, 0).astype(BF).T
-
-    def swap(first, count):
+            if w == 1:
+                z_sends.append(z_stage(p - 1 if p else 4))
+
+    def group(g):
+        return pl.ds(3 * g, 3 if g < 4 else 4)
+
+    def swap(g):
         return pltpu.make_async_remote_copy(
-            src_ref=gw_ref.at[pl.ds(first, count), :, 1 - core], dst_ref=r0_ref.at[pl.ds(first, count)],
-            send_sem=rs_send.at[first], recv_sem=rs_recv.at[first],
+            src_ref=gw_ref.at[group(g), 1 - core], dst_ref=r0_ref.at[group(g)],
+            send_sem=rs_send.at[g], recv_sem=rs_recv.at[g],
             device_id=chip(*at, 1 - core), device_id_type=MESH)
 
-    tr_ref[0] = nbf_ref[...].T
-    tr_ref[1] = att_ref[...].T
-    for m in range(4):
-        block = pltpu.roll(dot(tr_ref[1], cw_ref[:, pl.ds(128 * m, 128)]), 64, 1)
-        gw_ref[12 + m] = block.reshape(8, 2, 32, 128)
-    swaps = [swap(12, 4)]
-    swaps[0].start()
-    for p in range(4):
-        backward(p)
-        pieces = jnp.concatenate([gp_ref[:, pl.ds(512 * t + 128 * p, 128)] for t in range(3)], 1)
-        grads = dot(tr_ref[0], pieces)
-        for t in range(3):
-            gw_ref[4 * t + p] = grads[:, 128 * t:128 * t + 128].reshape(8, 2, 32, 128)
-            swaps.append(swap(4 * t + p, 1))
-            swaps[-1].start()
-
-    for w in range(4):
+    def z_stage(g):
+        swaps[g].wait_recv()
+        for b in range(3 * g, 3 * g + (3 if g < 4 else 4)):
+            zs_ref[b] = (gw_ref[b, core] + r0_ref[b]).astype(BF).reshape(2, 4, 32, 128)
+        copies = []
+        for k in (1, 2, 3):
+            n = 2 + 3 * g + k
+            copies.append(pltpu.make_async_remote_copy(
+                src_ref=zs_ref.at[group(g), :, (at[2] + k) % 4], dst_ref=zr_ref.at[k - 1, group(g)],
+                send_sem=rs_send.at[n + 2], recv_sem=rs_recv.at[n + 2],
+                device_id=ahead(0, 0, k), device_id_type=MESH))
+            copies[-1].start()
+        return copies
+
+    def gradient(w):
         rows = pl.ds(w * SPAN, SPAN)
         gh = dot(gp_ref[rows, :], w_ref[...], NT) * gain
         normed = normed_ref[rows, :]
         gs = inv_ref[rows, :] * (gh - jnp.mean(gh, -1, keepdims=True)
                                  - normed * jnp.mean(gh * normed, -1, keepdims=True))
         nbf_ref[rows, :] = gs.astype(BF)
-    for copy in swaps:
-        copy.wait_recv()
+
+    tr_ref[0] = nbf_ref[...].T
+    tr_ref[1] = att_ref[...].T
+    swaps = {g: swap(g) for g in range(5)}
+    z_sends = []
+
+    def keep(b, grads):
+        halves = grads.reshape(8, 2, 32, 128)
+        gw_ref[b, 0] = halves[:, 0]
+        gw_ref[b, 1] = halves[:, 1]
+
     for m in range(4):
-        whole = [gw_ref[b, :, core] + r0_ref[b] for b in (3 * m, 3 * m + 1, 3 * m + 2, 12 + m)]
-        left = lane < 64
+        keep(12 + m, pltpu.roll(dot(tr_ref[1], cw_ref[:, pl.ds(128 * m, 128)]), 64, 1))
+    swaps[4].start()
+    for p in range(4):
+        backward(p)
+        pieces = jnp.concatenate([gp_ref[:, pl.ds(512 * t + 128 * p, 128)] for t in range(3)], 1)
+        grads = dot(tr_ref[0], pieces)
+        for t in range(3):
+            keep(3 * p + t, grads[:, 128 * t:128 * t + 128])
+        swaps[p].start()
+
+    for w in range(3):
+        gradient(w)
+    z_sends.append(z_stage(3))
+    gradient(3)
+    pg_ref[...] = dot(unwindow_ref[...], nbf_ref[...]).astype(BF)
+    go_grad = halo(3, pg_ref, rg_ref, True)
+    for copy in go_grad:
+        copy.start()
+    rg_ref[pl.ds(0, 224), :] = pg_ref[pl.ds(0, 224), :]
+
+    for copies in z_sends:
+        for copy in copies:
+            copy.wait_recv()
+
+    def summed(b):
+        total = zs_ref[b, :, at[2]].astype(F32)
+        for k in range(3):
+            total = total + zr_ref[k, b].astype(F32)
+        return total
+
+    left = lane < 64
+    for m in range(4):
+        whole = [summed(b % 4 * 3 + b // 4) for b in (3 * m, 3 * m + 1, 3 * m + 2)] + [summed(12 + m)]
         for n, parts in ((0, (whole[0], jnp.where(left, whole[1], whole[3]))),
                          (1, (whole[2], jnp.where(left, whole[3], whole[1])))):
             for half in range(2):
                 for x_lo in range(2):
-                    s0_ref[m // 2 * 2 + x_lo, m % 2 * 2 + n, :, half] = parts[half][4 * x_lo:4 * x_lo + 4].astype(BF)
-
-    def scatter(stage, s, k, src, dst):
-        n = 16 + (stage * 4 + s) * 3 + k - 1
-        return pltpu.make_async_remote_copy(
-            src_ref=src, dst_ref=dst, send_sem=rs_send.at[n], recv_sem=rs_recv.at[n],
-            device_id=along(ORDERS[s][stage], k), device_id_type=MESH)
-
-    def quarter(s, axis, index):
-        half, rows = s // 2, pl.ds(s % 2 * 16, 16)
-        if axis == 0:
-            return s0_ref.at[index, :, :, half, rows]
-        if axis == 1:
-            return s0_ref.at[:, index, :, half, rows]
-        return s0_ref.at[:, :, index, half, rows]
-
-    first = [[scatter(0, s, k, quarter(s, ORDERS[s][0], (at[ORDERS[s][0]] + k) % 4), r1_ref.at[s, k - 1])
-              for k in (1, 2, 3)] for s in range(4)]
-    for k in range(3):
-        for s in range(4):
-            first[s][k].start()
-    pg_ref[...] = dot(unwindow_ref[...], nbf_ref[...]).astype(BF)
-    go_grad = halo(3, pg_ref, rg_ref, True)
-    for copy in go_grad:
-        copy.start()
-    rg_ref[pl.ds(0, 224), :] = pg_ref[pl.ds(0, 224), :]
+                    ps_ref[m // 2 * 2 + x_lo, m % 2 * 2 + n, half] = parts[half][x_lo]
+    planes = []
+    for n, (dx, dy) in enumerate(steps):
+        planes.append(pltpu.make_async_remote_copy(
+            src_ref=ps_ref.at[(at[0] + dx) % 4, (at[1] + dy) % 4], dst_ref=pr_ref.at[n],
+            send_sem=rs_send.at[20 + n], recv_sem=rs_recv.at[20 + n],
+            device_id=ahead(dx, dy, 0), device_id_type=MESH))
+    for copy in planes:
+        copy.start()
 
     loads[7].wait()
     for copy in go_out:
         copy.wait_recv()
     result_ref[...] = dot(unpack_ref[...], ro_ref[...]).astype(BF)
 
-    second = []
-    for s in range(4):
-        axis, nxt = ORDERS[s][0], ORDERS[s][1]
-        for copy in first[s]:
-            copy.wait_recv()
-        total = quarter(s, axis, at[axis])[...].astype(F32)
-        for k in range(3):
-            total = total + r1_ref[s, k].astype(F32)
-        s1_ref[s] = total
-        copies = []
-        for k in (1, 2, 3):
-            there = (at[nxt] + k) % 4
-            left = [a for a in range(3) if a != axis]
-            src = s1_ref.at[s, there] if left[0] == nxt else s1_ref.at[s, :, there]
-            copies.append(scatter(1, s, k, src, r2_ref.at[s, k - 1]))
-            copies[-1].start()
-        second.append(copies)
-    third = []
-    for s in range(4):
-        axis, nxt, last = ORDERS[s]
-        for copy in second[s]:
-            copy.wait_recv()
-        left = [a for a in range(3) if a != axis]
-        total = s1_ref[s, at[nxt]] if left[0] == nxt else s1_ref[s, :, at[nxt]]
-        for k in range(3):
-            total = total + r2_ref[s, k]
-        s2_ref[s] = total
-        copies = []
-        for k in (1, 2, 3):
-            copies.append(scatter(2, s, k, s2_ref.at[s, (at[last] + k) % 4], r3_ref.at[s, k - 1]))
-            copies[-1].start()
-        third.append(copies)
     for copy in go_grad:
         copy.wait_recv()
     grad_ref[...] = (cot_ref[...].astype(F32) + dot(unpack_ref[...], rg_ref[...])).astype(BF)
-    for s in range(4):
-        for copy in third[s]:
-            copy.wait_recv()
-        total = s2_ref[s, at[ORDERS[s][2]]]
-        for k in range(3):
-            total = total + r3_ref[s, k]
-        fin_ref[pl.ds(s % 2 * 16, 16), pl.ds(s // 2 * 128, 128)] = total
+    for copy in planes:
+        copy.wait_recv()
+    total = ps_ref[at[0], at[1]]
+    for n in range(15):
+        total = total + pr_ref[n]
+    fin_ref[...] = total
     last = pltpu.make_async_remote_copy(
-        src_ref=fin_ref, dst_ref=all_ref.at[core], send_sem=rs_send.at[52], recv_sem=rs_recv.at[52],
+        src_ref=fin_ref, dst_ref=all_ref.at[core], send_sem=rs_send.at[35], recv_sem=rs_recv.at[35],
         device_id=chip(*at, 1 - core), device_id_type=MESH)
     last.start()
     all_ref[core] = fin_ref[...]
     last.wait_recv()
-    whole = all_ref[...].reshape(64, 256)
+    whole = jnp.concatenate([all_ref[:, half].reshape(64, 128) for half in range(2)], 1)
     whole = jnp.where(at[1] % 2 == 1, pltpu.roll(whole, 64, 1), whole)
     gq_ref[...] = jnp.where(core == 1, pltpu.roll(whole, 160, 1), whole)[:, :96]
     outs = whole[:, 128:]
     go_ref[...] = jnp.where(core == 1, pltpu.roll(outs, 32, 1), pltpu.roll(outs, 64, 1)).T[:32]
 
-    started = go_x + go_regions + go_cot + go_out + go_grad + swaps + [last]
-    for copies in first + second + third:
+    started = go_x + go_regions + go_cot + go_out + go_grad + list(swaps.values()) + planes + [last]
+    for copies in z_sends:
         started += copies
     for copy in started:
         copy.wait_send()
 
 
 def hand_over(*refs):
-    copies = [pltpu.make_async_copy(refs[n], refs[4 + n], refs[8].at[n]) for n in range(4)]
-    for copy in copies:
-        copy.start()
-    for copy in copies:
-        copy.wait()
+    for n in range(4):
+        refs[4 + n][...] = refs[n][...]
 
 
 def on_device(tokens, cotangent, region_ids, norm_gain, qkv_weight, out_weight):
@@ -413,13 +402,12 @@
             bf(TOKENS, 3 * WIDTH), f32(4, 4, 2, SPAN, SPAN), bf(TOKENS, WIDTH), bf(TOKENS, WIDTH),
             bf(TOKENS, 3 * WIDTH), bf(2, WIDTH, TOKENS),
             bf(PACKED, WIDTH), bf(PACKED, WIDTH), bf(PACKED, WIDTH), bf(PACKED, WIDTH),
-            f32(16, 8, 2, 32, 128), f32(16, 8, 32, 128), bf(4, 4, 4, 2, 32, 128),
-            bf(4, 3, 4, 4, 16, 128), f32(4, 4, 4, 16, 128),
-            f32(4, 3, 4, 16, 128), f32(4, 4, 16, 128), f32(4, 3, 16, 128), f32(32, 256), f32(2, 32, 256),
+            f32(16, 2, 8, 32, 128), f32(16, 8, 32, 128), bf(16, 2, 4, 32, 128), bf(3, 16, 2, 32, 128),
+            f32(4, 4, 2, 32, 128), f32(15, 2, 32, 128), f32(2, 32, 128), f32(2, 2, 32, 128),
             pltpu.SemaphoreType.DMA((8,)),
             pltpu.SemaphoreType.DMA((4, 6)), pltpu.SemaphoreType.DMA((4, 6)),
             pltpu.SemaphoreType.DMA((2,)), pltpu.SemaphoreType.DMA((2,)),
-            pltpu.SemaphoreType.DMA((53,)), pltpu.SemaphoreType.DMA((53,)),
+            pltpu.SemaphoreType.DMA((36,)), pltpu.SemaphoreType.DMA((36,)),
         ],
         compiler_params=pltpu.CompilerParams(
             vmem_limit_bytes=56 << 20, collective_id=0, has_side_effects=True),
@@ -431,9 +419,8 @@
     result, grad, gq, go = pl.pallas_call(
         hand_over,
         out_shape=tuple(jax.ShapeDtypeStruct(a.shape, a.dtype) for a in sums),
-        in_specs=[hbm] * 4,
-        out_specs=(hbm,) * 4,
-        scratch_shapes=[pltpu.SemaphoreType.DMA((4,))],
+        in_specs=[vm] * 4,
+        out_specs=(vm,) * 4,
     )(*sums)
     return (result.reshape(tokens.shape), grad.reshape(tokens.shape), gq, go.T)
 

time: 97.1 us -> 63.4 us (0.65)
  Pallas kernels: 96.1 us -> 62.6 us
    pallas_call x1, Pallas kernels: 38.4 us -> 2.3 us  [on_device(): pl.pallas_call(hand_over, out_shape=tuple((jax.ShapeDtypeStruct(a.shape,...]
    pallas_call x1, Pallas kernels: 57.8 us -> 60.3 us  [on_device(): pl.pallas_call(kernel, out_shape=(jax.ShapeDtypeStruct((TOKENS, WIDTH), B...]
where the time goes in v4:
time: 63.4 us; the launch traced here: 63.2 us
  Pallas kernels  62.6 us (99%)
  between operations  0.64 us (1%)
    pallas_call x1, Pallas kernels, on_device(): pl.pallas_call(kernel, out_shape=(jax.ShapeDtypeStruct((TOKENS, WIDTH), B...  60.3 us
    pallas_call x1, Pallas kernels, on_device(): pl.pallas_call(hand_over, out_shape=tuple((jax.ShapeDtypeStruct(a.shape,...  2.3 us

profile of v4, /device:TPU:1, one launch (start us, length us, event | category | flops | bytes accessed | tf_op | source)
XLA Modules:
  0.0 63.2 jit_solution(8669228952821663335)
XLA Ops:
  0.6 60.3 %shard_map.147 = (bf16[576,512]{1,0:T(8,128)(2,1)}, bf16[576,512]{1,0:T(8,128)(2,1)}, f32[64,96]{1,0:T(8,128)}, f32[32,64]{1,0:T(8,128)}) custom-call(bf16[576,512]{1,0:T(8,128)(2,1)} %bitcast.7, bf16[576,512]{1,0:T(8,128)(2,1)} %bitcast.8, s32[6,4,24]{2,1,0:T(4,128)} %bitcast.12, f32[1,512]{1,0:T(1,128)} %bitcast.13, bf16[512,1536]{1,0:T(8,128)(2,1)} %w_hbm.1, ...), custom_call_target="tpu_custom_call" | custom-call | flops 6000000000 | bytes 10000000 | tf_op jit(solution)/shard_map/pallas_call | solution.py:386
  60.9 2.3 %shard_map.148 = (bf16[576,512]{1,0:T(8,128)(2,1)}, bf16[576,512]{1,0:T(8,128)(2,1)}, f32[64,96]{1,0:T(8,128)}, f32[32,64]{1,0:T(8,128)}) custom-call(bf16[576,512]{1,0:T(8,128)(2,1)} %get-tuple-element.12.refs_0_, bf16[576,512]{1,0:T(8,128)(2,1)} %get-tuple-element.13.refs_1_, f32[64,96]{1,0:T(8,128)} %get-tuple-element.14.refs_2_, ...), custom_call_target="tpu_custom_call" | custom-call | tf_op jit(solution)/shard_map/pallas_call | solution.py:419

commit v5 on v4

--- a/solution.py
+++ b/solution.py
@@ -68,13 +68,13 @@
 
 def kernel(x_hbm, cot_hbm, region_ref, gain_ref, w_hbm, wo_hbm,
            pack_hbm, window_hbm, unpack_hbm, unwindow_hbm, row_ref, column_ref,
-           result_ref, grad_ref, gq_ref, go_ref,
+           result_hbm, grad_hbm, gq_ref, go_ref,
            x_ref, cot_ref, w_ref, wo_ref, pack_ref, window_ref, unpack_ref, unwindow_ref,
            px_ref, pc_ref, rx_ref, rc_ref, regions_ref, rr_ref, hot_ref,
            xw_ref, cw_ref, normed_ref, nbf_ref, inv_ref, proj_ref, aw_ref, att_ref, ga_ref, gp_ref, tr_ref,
            po_ref, pg_ref, ro_ref, rg_ref,
-           gw_ref, r0_ref, zs_ref, zr_ref, ps_ref, pr_ref, fin_ref, all_ref,
-           load_sem, halo_send, halo_recv, region_send, region_recv, rs_send, rs_recv):
+           gw_ref, r0_ref, zs_ref, zr_ref, ps_ref, pr_ref, fin_ref, all_ref, result_ref, grad_ref,
+           load_sem, halo_send, halo_recv, region_send, region_recv, rs_send, rs_recv, out_sem):
     lat, lon = lax.axis_index("lat"), lax.axis_index("lon")
     core = lon % 2
     at = (lon // 8 * 2 + lat // 4, lon // 2 % 4, lat % 4)
@@ -119,10 +119,16 @@
 
     loads[0].wait()
     loads[1].wait()
-    px_ref[...] = dot(pack_ref[...], x_ref[...]).astype(BF)
+    def packed(src, dst, row, rows):
+        dst[pl.ds(row, rows), :] = dot(pack_ref[pl.ds(row, rows), :], src[...]).astype(BF)
+
+    go_x = halo(0, px_ref, rx_ref, False)
+    packed(x_ref, px_ref, 224, 224)
     pl.semaphore_wait(barrier, len(partners))
-    go_x = halo(0, px_ref, rx_ref, False)
-    for copy in go_x:
+    for copy in go_x[:2]:
+        copy.start()
+    packed(x_ref, px_ref, 448, 192)
+    for copy in go_x[2:]:
         copy.start()
     go_regions = [
         pltpu.make_async_remote_copy(
@@ -134,12 +140,12 @@
     for copy in go_regions:
         copy.start()
     loads[2].wait()
-    pc_ref[...] = dot(pack_ref[...], cot_ref[...]).astype(BF)
     go_cot = halo(1, pc_ref, rc_ref, False)
+    packed(cot_ref, pc_ref, 224, 416)
     for copy in go_cot:
         copy.start()
-    rx_ref[pl.ds(0, 224), :] = px_ref[pl.ds(0, 224), :]
-    rc_ref[pl.ds(0, 224), :] = pc_ref[pl.ds(0, 224), :]
+    packed(x_ref, rx_ref, 0, 224)
+    packed(cot_ref, rc_ref, 0, 224)
 
     for copy in go_regions:
         copy.wait_recv()
@@ -297,59 +303,84 @@
             keep(3 * p + t, grads[:, 128 * t:128 * t + 128])
         swaps[p].start()
 
-    for w in range(3):
-        gradient(w)
-    z_sends.append(z_stage(3))
-    gradient(3)
-    pg_ref[...] = dot(unwindow_ref[...], nbf_ref[...]).astype(BF)
-    go_grad = halo(3, pg_ref, rg_ref, True)
-    for copy in go_grad:
-        copy.start()
-    rg_ref[pl.ds(0, 224), :] = pg_ref[pl.ds(0, 224), :]
-
-    for copies in z_sends:
-        for copy in copies:
-            copy.wait_recv()
-
     def summed(b):
         total = zs_ref[b, :, at[2]].astype(F32)
         for k in range(3):
             total = total + zr_ref[k, b].astype(F32)
         return total
 
-    left = lane < 64
-    for m in range(4):
-        whole = [summed(b % 4 * 3 + b // 4) for b in (3 * m, 3 * m + 1, 3 * m + 2)] + [summed(12 + m)]
-        for n, parts in ((0, (whole[0], jnp.where(left, whole[1], whole[3]))),
-                         (1, (whole[2], jnp.where(left, whole[3], whole[1])))):
-            for half in range(2):
+    def place(pairs):
+        for copies in [z_sends[p + 1] for p in pairs] + (z_sends[:1] if 0 in pairs else []):
+            for copy in copies:
+                copy.wait_recv()
+        for b in range(12):
+            if b % 4 not in pairs:
+                continue
+            m, whole = b // 3, summed(b % 4 * 3 + b // 4)
+            if b % 3 == 1:
+                out = summed(12 + m)
+                targets = ((0, 1, jnp.where(lane < 64, whole, out)), (1, 1, jnp.where(lane < 64, out, whole)))
+            else:
+                targets = ((b % 3 // 2, 0, whole),)
+            for n, half, part in targets:
                 for x_lo in range(2):
-                    ps_ref[m // 2 * 2 + x_lo, m % 2 * 2 + n, half] = parts[half][x_lo]
+                    ps_ref[m // 2 * 2 + x_lo, m % 2 * 2 + n, half] = part[x_lo]
+
     planes = []
     for n, (dx, dy) in enumerate(steps):
-        planes.append(pltpu.make_async_remote_copy(
-            src_ref=ps_ref.at[(at[0] + dx) % 4, (at[1] + dy) % 4], dst_ref=pr_ref.at[n],
-            send_sem=rs_send.at[20 + n], recv_sem=rs_recv.at[20 + n],
-            device_id=ahead(dx, dy, 0), device_id_type=MESH))
-    for copy in planes:
-        copy.start()
+        planes.append([pltpu.make_async_remote_copy(
+            src_ref=ps_ref.at[(at[0] + dx) % 4, (at[1] + dy) % 4, half], dst_ref=pr_ref.at[n, half],
+            send_sem=rs_send.at[20 + 2 * n + half], recv_sem=rs_recv.at[20 + 2 * n + half],
+            device_id=ahead(dx, dy, 0), device_id_type=MESH) for half in range(2)])
+
+    def start_if(n, half, early):
+        x_hi, y = (at[0] + steps[n][0]) % 4 // 2, (at[1] + steps[n][1]) % 4
+        first = x_hi == (0 if half else (y + 1) % 4 // 2)
+
+        @pl.when(first if early else jnp.logical_not(first))
+        def _():
+            planes[n][half].start()
+
+    place((0, 1))
+    for half in range(2):
+        for n in range(15):
+            start_if(n, half, True)
+
+    z_sends.append(z_stage(3))
+    for w in range(4):
+        gradient(w)
+    pg_ref[...] = dot(unwindow_ref[...], nbf_ref[...]).astype(BF)
+    go_grad = halo(3, pg_ref, rg_ref, True)
+    for copy in go_grad:
+        copy.start()
+    rg_ref[pl.ds(0, 224), :] = pg_ref[pl.ds(0, 224), :]
+
+    place((2, 3))
+    for half in range(2):
+        for n in range(15):
+            start_if(n, half, False)
 
     loads[7].wait()
     for copy in go_out:
         copy.wait_recv()
     result_ref[...] = dot(unpack_ref[...], ro_ref[...]).astype(BF)
+    outs = [pltpu.make_async_copy(result_ref, result_hbm, out_sem.at[0]),
+            pltpu.make_async_copy(grad_ref, grad_hbm, out_sem.at[1])]
+    outs[0].start()
 
     for copy in go_grad:
         copy.wait_recv()
     grad_ref[...] = (cot_ref[...].astype(F32) + dot(unpack_ref[...], rg_ref[...])).astype(BF)
-    for copy in planes:
-        copy.wait_recv()
+    outs[1].start()
+    for copies in planes:
+        for copy in copies:
+            copy.wait_recv()
     total = ps_ref[at[0], at[1]]
     for n in range(15):
         total = total + pr_ref[n]
     fin_ref[...] = total
     last = pltpu.make_async_remote_copy(
-        src_ref=fin_ref, dst_ref=all_ref.at[core], send_sem=rs_send.at[35], recv_sem=rs_recv.at[35],
+        src_ref=fin_ref, dst_ref=all_ref.at[core], send_sem=rs_send.at[50], recv_sem=rs_recv.at[50],
         device_id=chip(*at, 1 - core), device_id_type=MESH)
     last.start()
     all_ref[core] = fin_ref[...]
@@ -357,14 +388,16 @@
     whole = jnp.concatenate([all_ref[:, half].reshape(64, 128) for half in range(2)], 1)
     whole = jnp.where(at[1] % 2 == 1, pltpu.roll(whole, 64, 1), whole)
     gq_ref[...] = jnp.where(core == 1, pltpu.roll(whole, 160, 1), whole)[:, :96]
-    outs = whole[:, 128:]
-    go_ref[...] = jnp.where(core == 1, pltpu.roll(outs, 32, 1), pltpu.roll(outs, 64, 1)).T[:32]
-
-    started = go_x + go_regions + go_cot + go_out + go_grad + list(swaps.values()) + planes + [last]
-    for copies in z_sends:
+    ours = whole[:, 128:]
+    go_ref[...] = jnp.where(core == 1, pltpu.roll(ours, 32, 1), pltpu.roll(ours, 64, 1)).T[:32]
+
+    started = go_x + go_regions + go_cot + go_out + go_grad + list(swaps.values()) + [last]
+    for copies in z_sends + planes:
         started += copies
     for copy in started:
         copy.wait_send()
+    for copy in outs:
+        copy.wait()
 
 
 def hand_over(*refs):
@@ -392,7 +425,7 @@
             jax.ShapeDtypeStruct((32, 64), F32),
         ),
         in_specs=[hbm, hbm, vm, vm, hbm, hbm, hbm, hbm, hbm, hbm, vm, vm],
-        out_specs=(vm, vm, vm, vm),
+        out_specs=(hbm, hbm, vm, vm),
         scratch_shapes=[
             bf(TOKENS, WIDTH), bf(TOKENS, WIDTH), bf(WIDTH, 3 * WIDTH), bf(WIDTH, WIDTH),
             bf(PACKED, TOKENS), bf(TOKENS, PACKED), bf(TOKENS, PACKED), bf(PACKED, TOKENS),
@@ -404,10 +437,12 @@
             bf(PACKED, WIDTH), bf(PACKED, WIDTH), bf(PACKED, WIDTH), bf(PACKED, WIDTH),
             f32(16, 2, 8, 32, 128), f32(16, 8, 32, 128), bf(16, 2, 4, 32, 128), bf(3, 16, 2, 32, 128),
             f32(4, 4, 2, 32, 128), f32(15, 2, 32, 128), f32(2, 32, 128), f32(2, 2, 32, 128),
+            bf(TOKENS, WIDTH), bf(TOKENS, WIDTH),
             pltpu.SemaphoreType.DMA((8,)),
             pltpu.SemaphoreType.DMA((4, 6)), pltpu.SemaphoreType.DMA((4, 6)),
             pltpu.SemaphoreType.DMA((2,)), pltpu.SemaphoreType.DMA((2,)),
-            pltpu.SemaphoreType.DMA((36,)), pltpu.SemaphoreType.DMA((36,)),
+            pltpu.SemaphoreType.DMA((51,)), pltpu.SemaphoreType.DMA((51,)),
+            pltpu.SemaphoreType.DMA((2,)),
         ],
         compiler_params=pltpu.CompilerParams(
             vmem_limit_bytes=56 << 20, collective_id=0, has_side_effects=True),

time: 63.4 us -> 58.8 us (0.927)
  the two profiles are of different devices: /device:TPU:1 before, /device:TPU:7 now
where the time goes in v5:
time: 58.8 us; the launch traced here: 58.6 us
  Pallas kernels  58 us (99%)
  between operations  0.64 us (1%)
    pallas_call x1, Pallas kernels, on_device(): pl.pallas_call(kernel, out_shape=(jax.ShapeDtypeStruct((TOKENS, WIDTH), B...  55.7 us
    pallas_call x1, Pallas kernels, on_device(): pl.pallas_call(hand_over, out_shape=tuple((jax.ShapeDtypeStruct(a.shape,...  2.3 us

profile of v5, /device:TPU:7, one launch (start us, length us, event | category | flops | bytes accessed | tf_op | source)
XLA Modules:
  0.0 58.6 jit_solution(6389008688055795744)
XLA Ops:
  0.6 55.7 %shard_map.147 = (bf16[576,512]{1,0:T(8,128)(2,1)}, bf16[576,512]{1,0:T(8,128)(2,1)}, f32[64,96]{1,0:T(8,128)}, f32[32,64]{1,0:T(8,128)}) custom-call(bf16[576,512]{1,0:T(8,128)(2,1)} %bitcast.7, bf16[576,512]{1,0:T(8,128)(2,1)} %bitcast.8, s32[6,4,24]{2,1,0:T(4,128)} %bitcast.12, f32[1,512]{1,0:T(1,128)} %bitcast.13, bf16[512,1536]{1,0:T(8,128)(2,1)} %w_hbm.1, ...), custom_call_target="tpu_custom_call" | custom-call | flops 6000000000 | bytes 10000000 | tf_op jit(solution)/shard_map/pallas_call | solution.py:419
  56.3 2.3 %shard_map.148 = (bf16[576,512]{1,0:T(8,128)(2,1)}, bf16[576,512]{1,0:T(8,128)(2,1)}, f32[64,96]{1,0:T(8,128)}, f32[32,64]{1,0:T(8,128)}) custom-call(bf16[576,512]{1,0:T(8,128)(2,1)} %get-tuple-element.12.refs_0_, bf16[576,512]{1,0:T(8,128)(2,1)} %get-tuple-element.13.refs_1_, f32[64,96]{1,0:T(8,128)} %get-tuple-element.14.refs_2_, ...), custom_call_target="tpu_custom_call" | custom-call | tf_op jit(solution)/shard_map/pallas_call | solution.py:454

commit v6 on v5

--- a/solution.py
+++ b/solution.py
@@ -66,9 +66,10 @@
     return lax.dot_general(a, b, dims, preferred_element_type=F32)
 
 
-def kernel(x_hbm, cot_hbm, region_ref, gain_ref, w_hbm, wo_hbm,
-           pack_hbm, window_hbm, unpack_hbm, unwindow_hbm, row_ref, column_ref,
+def kernel(x_hbm, cot_hbm, region_hbm, gain_hbm, w_hbm, wo_hbm,
+           pack_hbm, window_hbm, unpack_hbm, unwindow_hbm, row_hbm, column_hbm,
            result_hbm, grad_hbm, gq_ref, go_ref,
+           region_ref, gain_ref, row_ref, column_ref,
            x_ref, cot_ref, w_ref, wo_ref, pack_ref, window_ref, unpack_ref, unwindow_ref,
            px_ref, pc_ref, rx_ref, rc_ref, regions_ref, rr_ref, hot_ref,
            xw_ref, cw_ref, normed_ref, nbf_ref, inv_ref, proj_ref, aw_ref, att_ref, ga_ref, gp_ref, tr_ref,
@@ -98,10 +99,11 @@
         for n, (src, dst) in enumerate((
             (pack_hbm, pack_ref), (x_hbm, x_ref), (cot_hbm, cot_ref), (window_hbm, window_ref), (w_hbm, w_ref),
             (wo_hbm, wo_ref), (unwindow_hbm, unwindow_ref), (unpack_hbm, unpack_ref),
+            (region_hbm, region_ref), (row_hbm, row_ref), (column_hbm, column_ref), (gain_hbm, gain_ref),
         ))
     ]
-    for load in loads:
-        load.start()
+    for n in (0, 1, 2, 8, 9, 10, 11, 3, 4, 5, 6, 7):
+        loads[n].start()
 
     barrier = pltpu.get_barrier_semaphore()
     for partner in partners:
@@ -132,7 +134,7 @@
         copy.start()
     go_regions = [
         pltpu.make_async_remote_copy(
-            src_ref=region_ref, dst_ref=regions_ref.at[n],
+            src_ref=region_hbm, dst_ref=regions_ref.at[n],
             send_sem=region_send.at[n], recv_sem=region_recv.at[n],
             device_id=near(step), device_id_type=MESH)
         for n, step in enumerate(((-1, 0), (-1, -1)))
@@ -147,6 +149,8 @@
     packed(x_ref, rx_ref, 0, 224)
     packed(cot_ref, rc_ref, 0, 224)
 
+    for load in loads[8:]:
+        load.wait()
     for copy in go_regions:
         copy.wait_recv()
     rr_ref[...] = jnp.zeros_like(rr_ref)
@@ -205,17 +209,6 @@
         forward(p)
 
     loads[5].wait()
-    for w in range(4):
-        rows = pl.ds(w * SPAN, SPAN)
-        branch = dot(att_ref[rows, :], wo_ref[...])
-        xw_ref[rows, :] = (xw_ref[rows, :].astype(F32) + branch).astype(BF)
-    loads[6].wait()
-    po_ref[...] = dot(unwindow_ref[...], xw_ref[...]).astype(BF)
-    go_out = halo(2, po_ref, ro_ref, True)
-    for copy in go_out:
-        copy.start()
-    ro_ref[pl.ds(0, 224), :] = po_ref[pl.ds(0, 224), :]
-
     for copy in go_cot:
         copy.wait_recv()
     cw_ref[...] = dot(window_ref[...], rc_ref[...]).astype(BF)
@@ -333,32 +326,46 @@
             send_sem=rs_send.at[20 + 2 * n + half], recv_sem=rs_recv.at[20 + 2 * n + half],
             device_id=ahead(dx, dy, 0), device_id_type=MESH) for half in range(2)])
 
-    def start_if(n, half, early):
-        x_hi, y = (at[0] + steps[n][0]) % 4 // 2, (at[1] + steps[n][1]) % 4
-        first = x_hi == (0 if half else (y + 1) % 4 // 2)
-
-        @pl.when(first if early else jnp.logical_not(first))
-        def _():
-            planes[n][half].start()
-
-    place((0, 1))
-    for half in range(2):
-        for n in range(15):
-            start_if(n, half, True)
+    def exchange(pairs):
+        place(pairs)
+        for half in range(2):
+            for n in range(15):
+                x_hi, y = (at[0] + steps[n][0]) % 4 // 2, (at[1] + steps[n][1]) % 4
+                first = x_hi == (0 if half else (y + 1) % 4 // 2)
+                low = y < 2
+                if 0 in pairs:
+                    mine = first
+                elif 2 in pairs:
+                    mine = jnp.logical_and(jnp.logical_not(first), jnp.logical_not(low) if half else low)
+                else:
+                    mine = jnp.logical_and(jnp.logical_not(first), low if half else jnp.logical_not(low))
+                pl.when(mine)(planes[n][half].start)
+
+    exchange((0, 1))
 
     z_sends.append(z_stage(3))
     for w in range(4):
-        gradient(w)
+        rows = pl.ds(w * SPAN, SPAN)
+        branch = dot(att_ref[rows, :], wo_ref[...])
+        xw_ref[rows, :] = (xw_ref[rows, :].astype(F32) + branch).astype(BF)
+    loads[6].wait()
+    po_ref[...] = dot(unwindow_ref[...], xw_ref[...]).astype(BF)
+    go_out = halo(2, po_ref, ro_ref, True)
+    for copy in go_out:
+        copy.start()
+    ro_ref[pl.ds(0, 224), :] = po_ref[pl.ds(0, 224), :]
+    gradient(0)
+    gradient(1)
+    exchange((2,))
+    gradient(2)
+    gradient(3)
     pg_ref[...] = dot(unwindow_ref[...], nbf_ref[...]).astype(BF)
     go_grad = halo(3, pg_ref, rg_ref, True)
     for copy in go_grad:
         copy.start()
     rg_ref[pl.ds(0, 224), :] = pg_ref[pl.ds(0, 224), :]
 
-    place((2, 3))
-    for half in range(2):
-        for n in range(15):
-            start_if(n, half, False)
+    exchange((3,))
 
     loads[7].wait()
     for copy in go_out:
@@ -424,9 +431,10 @@
             jax.ShapeDtypeStruct((64, 96), F32),
             jax.ShapeDtypeStruct((32, 64), F32),
         ),
-        in_specs=[hbm, hbm, vm, vm, hbm, hbm, hbm, hbm, hbm, hbm, vm, vm],
+        in_specs=[hbm] * 12,
         out_specs=(hbm, hbm, vm, vm),
         scratch_shapes=[
+            pltpu.VMEM((6, 4, 24), jnp.int32), f32(1, WIDTH), bf(TOKENS, 144), bf(TOKENS, 128),
             bf(TOKENS, WIDTH), bf(TOKENS, WIDTH), bf(WIDTH, 3 * WIDTH), bf(WIDTH, WIDTH),
             bf(PACKED, TOKENS), bf(TOKENS, PACKED), bf(TOKENS, PACKED), bf(PACKED, TOKENS),
             bf(PACKED, WIDTH), bf(PACKED, WIDTH), bf(PACKED, WIDTH), bf(PACKED, WIDTH),
@@ -438,7 +446,7 @@
             f32(16, 2, 8, 32, 128), f32(16, 8, 32, 128), bf(16, 2, 4, 32, 128), bf(3, 16, 2, 32, 128),
             f32(4, 4, 2, 32, 128), f32(15, 2, 32, 128), f32(2, 32, 128), f32(2, 2, 32, 128),
             bf(TOKENS, WIDTH), bf(TOKENS, WIDTH),
-            pltpu.SemaphoreType.DMA((8,)),
+            pltpu.SemaphoreType.DMA((12,)),
             pltpu.SemaphoreType.DMA((4, 6)), pltpu.SemaphoreType.DMA((4, 6)),
             pltpu.SemaphoreType.DMA((2,)), pltpu.SemaphoreType.DMA((2,)),
             pltpu.SemaphoreType.DMA((51,)), pltpu.SemaphoreType.DMA((51,)),

time: 58.8 us -> 61.5 us (1.046)
  the two profiles are of different devices: /device:TPU:7 before, /device:TPU:1 now
where the time goes in v6:
time: 61.5 us; the launch traced here: 60.6 us
  Pallas kernels  59.9 us (97%)
  between operations  0.64 us (1%)
    pallas_call x1, Pallas kernels, on_device(): pl.pallas_call(kernel, out_shape=(jax.ShapeDtypeStruct((TOKENS, WIDTH), B...  57.6 us
    pallas_call x1, Pallas kernels, on_device(): pl.pallas_call(hand_over, out_shape=tuple((jax.ShapeDtypeStruct(a.shape,...  2.3 us

profile of v6, /device:TPU:1, one launch (start us, length us, event | category | flops | bytes accessed | tf_op | source)
XLA Modules:
  0.0 60.6 jit_solution(15341652859144795906)
XLA Ops:
  0.6 57.6 %shard_map.147 = (bf16[576,512]{1,0:T(8,128)(2,1)}, bf16[576,512]{1,0:T(8,128)(2,1)}, f32[64,96]{1,0:T(8,128)}, f32[32,64]{1,0:T(8,128)}) custom-call(bf16[576,512]{1,0:T(8,128)(2,1)} %bitcast.7, bf16[576,512]{1,0:T(8,128)(2,1)} %bitcast.8, s32[6,4,24]{2,1,0:T(4,128)} %bitcast.12, f32[1,512]{1,0:T(1,128)} %bitcast.13, bf16[512,1536]{1,0:T(8,128)(2,1)} %w_hbm.1, ...), custom_call_target="tpu_custom_call" | custom-call | flops 6000000000 | bytes 10000000 | tf_op jit(solution)/shard_map/pallas_call | solution.py:426
  58.3 2.3 %shard_map.148 = (bf16[576,512]{1,0:T(8,128)(2,1)}, bf16[576,512]{1,0:T(8,128)(2,1)}, f32[64,96]{1,0:T(8,128)}, f32[32,64]{1,0:T(8,128)}) custom-call(bf16[576,512]{1,0:T(8,128)(2,1)} %get-tuple-element.12.refs_0_, bf16[576,512]{1,0:T(8,128)(2,1)} %get-tuple-element.13.refs_1_, f32[64,96]{1,0:T(8,128)} %get-tuple-element.14.refs_2_, ...), custom_call_target="tpu_custom_call" | custom-call | tf_op jit(solution)/shard_map/pallas_call | solution.py:462

commit v7 on v6

--- a/solution.py
+++ b/solution.py
@@ -130,7 +130,7 @@
     for copy in go_x[:2]:
         copy.start()
     packed(x_ref, px_ref, 448, 192)
-    for copy in go_x[2:]:
+    for copy in go_x[4:] + go_x[2:4]:
         copy.start()
     go_regions = [
         pltpu.make_async_remote_copy(
@@ -144,7 +144,7 @@
     loads[2].wait()
     go_cot = halo(1, pc_ref, rc_ref, False)
     packed(cot_ref, pc_ref, 224, 416)
-    for copy in go_cot:
+    for copy in go_cot[4:] + go_cot[:4]:
         copy.start()
     packed(x_ref, rx_ref, 0, 224)
     packed(cot_ref, rc_ref, 0, 224)
@@ -209,6 +209,17 @@
         forward(p)
 
     loads[5].wait()
+    for w in range(4):
+        rows = pl.ds(w * SPAN, SPAN)
+        branch = dot(att_ref[rows, :], wo_ref[...])
+        xw_ref[rows, :] = (xw_ref[rows, :].astype(F32) + branch).astype(BF)
+    loads[6].wait()
+    po_ref[...] = dot(unwindow_ref[...], xw_ref[...]).astype(BF)
+    go_out = halo(2, po_ref, ro_ref, True)
+    for copy in go_out[4:] + go_out[:4]:
+        copy.start()
+    ro_ref[pl.ds(0, 224), :] = po_ref[pl.ds(0, 224), :]
+
     for copy in go_cot:
         copy.wait_recv()
     cw_ref[...] = dot(window_ref[...], rc_ref[...]).astype(BF)
@@ -332,40 +343,20 @@
             for n in range(15):
                 x_hi, y = (at[0] + steps[n][0]) % 4 // 2, (at[1] + steps[n][1]) % 4
                 first = x_hi == (0 if half else (y + 1) % 4 // 2)
-                low = y < 2
-                if 0 in pairs:
-                    mine = first
-                elif 2 in pairs:
-                    mine = jnp.logical_and(jnp.logical_not(first), jnp.logical_not(low) if half else low)
-                else:
-                    mine = jnp.logical_and(jnp.logical_not(first), low if half else jnp.logical_not(low))
+                mine = first if 0 in pairs else jnp.logical_not(first)
                 pl.when(mine)(planes[n][half].start)
 
-    exchange((0, 1))
-
-    z_sends.append(z_stage(3))
-    for w in range(4):
-        rows = pl.ds(w * SPAN, SPAN)
-        branch = dot(att_ref[rows, :], wo_ref[...])
-        xw_ref[rows, :] = (xw_ref[rows, :].astype(F32) + branch).astype(BF)
-    loads[6].wait()
-    po_ref[...] = dot(unwindow_ref[...], xw_ref[...]).astype(BF)
-    go_out = halo(2, po_ref, ro_ref, True)
-    for copy in go_out:
-        copy.start()
-    ro_ref[pl.ds(0, 224), :] = po_ref[pl.ds(0, 224), :]
     gradient(0)
     gradient(1)
-    exchange((2,))
     gradient(2)
+    z_sends.append(z_stage(3))
+    exchange((0, 1))
     gradient(3)
     pg_ref[...] = dot(unwindow_ref[...], nbf_ref[...]).astype(BF)
     go_grad = halo(3, pg_ref, rg_ref, True)
-    for copy in go_grad:
+    for copy in go_grad[4:] + go_grad[:4]:
         copy.start()
     rg_ref[pl.ds(0, 224), :] = pg_ref[pl.ds(0, 224), :]
-
-    exchange((3,))
 
     loads[7].wait()
     for copy in go_out:
@@ -374,6 +365,8 @@
     outs = [pltpu.make_async_copy(result_ref, result_hbm, out_sem.at[0]),
             pltpu.make_async_copy(grad_ref, grad_hbm, out_sem.at[1])]
     outs[0].start()
+
+    exchange((2, 3))
 
     for copy in go_grad:
         copy.wait_recv()

time: 61.5 us -> 58.3 us (0.948)
  the two profiles are of different devices: /device:TPU:1 before, /device:TPU:7 now
where the time goes in v7:
time: 58.3 us; the launch traced here: 58.1 us
  Pallas kernels  57.5 us (99%)
  between operations  0.64 us (1%)
    pallas_call x1, Pallas kernels, on_device(): pl.pallas_call(kernel, out_shape=(jax.ShapeDtypeStruct((TOKENS, WIDTH), B...  55.2 us
    pallas_call x1, Pallas kernels, on_device(): pl.pallas_call(hand_over, out_shape=tuple((jax.ShapeDtypeStruct(a.shape,...  2.3 us

profile of v7, /device:TPU:7, one launch (start us, length us, event | category | flops | bytes accessed | tf_op | source)
XLA Modules:
  0.0 58.1 jit_solution(143427011679914274)
XLA Ops:
  0.6 55.2 %shard_map.147 = (bf16[576,512]{1,0:T(8,128)(2,1)}, bf16[576,512]{1,0:T(8,128)(2,1)}, f32[64,96]{1,0:T(8,128)}, f32[32,64]{1,0:T(8,128)}) custom-call(bf16[576,512]{1,0:T(8,128)(2,1)} %bitcast.7, bf16[576,512]{1,0:T(8,128)(2,1)} %bitcast.8, s32[6,4,24]{2,1,0:T(4,128)} %bitcast.12, f32[1,512]{1,0:T(1,128)} %bitcast.13, bf16[512,1536]{1,0:T(8,128)(2,1)} %w_hbm.1, ...), custom_call_target="tpu_custom_call" | custom-call | flops 6000000000 | bytes 10000000 | tf_op jit(solution)/shard_map/pallas_call | solution.py:419
  55.8 2.3 %shard_map.148 = (bf16[576,512]{1,0:T(8,128)(2,1)}, bf16[576,512]{1,0:T(8,128)(2,1)}, f32[64,96]{1,0:T(8,128)}, f32[32,64]{1,0:T(8,128)}) custom-call(bf16[576,512]{1,0:T(8,128)(2,1)} %get-tuple-element.12.refs_0_, bf16[576,512]{1,0:T(8,128)(2,1)} %get-tuple-element.13.refs_1_, f32[64,96]{1,0:T(8,128)} %get-tuple-element.14.refs_2_, ...), custom_call_target="tpu_custom_call" | custom-call | tf_op jit(solution)/shard_map/pallas_call | solution.py:455

commit v8 on v7

--- a/solution.py
+++ b/solution.py
@@ -343,7 +343,13 @@
             for n in range(15):
                 x_hi, y = (at[0] + steps[n][0]) % 4 // 2, (at[1] + steps[n][1]) % 4
                 first = x_hi == (0 if half else (y + 1) % 4 // 2)
-                mine = first if 0 in pairs else jnp.logical_not(first)
+                low = y < 2
+                if 0 in pairs:
+                    mine = first
+                elif 2 in pairs:
+                    mine = jnp.logical_and(jnp.logical_not(first), jnp.logical_not(low) if half else low)
+                else:
+                    mine = jnp.logical_and(jnp.logical_not(first), low if half else jnp.logical_not(low))
                 pl.when(mine)(planes[n][half].start)
 
     gradient(0)
@@ -366,7 +372,8 @@
             pltpu.make_async_copy(grad_ref, grad_hbm, out_sem.at[1])]
     outs[0].start()
 
-    exchange((2, 3))
+    exchange((2,))
+    exchange((3,))
 
     for copy in go_grad:
         copy.wait_recv()

time: 58.3 us -> 57.2 us (0.981)
  the two profiles are of different devices: /device:TPU:7 before, /device:TPU:1 now
where the time goes in v8:
time: 57.2 us; the launch traced here: 56.8 us
  Pallas kernels  56.2 us (98%)
  between operations  0.64 us (1%)
    pallas_call x1, Pallas kernels, on_device(): pl.pallas_call(kernel, out_shape=(jax.ShapeDtypeStruct((TOKENS, WIDTH), B...  53.9 us
    pallas_call x1, Pallas kernels, on_device(): pl.pallas_call(hand_over, out_shape=tuple((jax.ShapeDtypeStruct(a.shape,...  2.3 us

profile of v8, /device:TPU:1, one launch (start us, length us, event | category | flops | bytes accessed | tf_op | source)
XLA Modules:
  0.0 56.8 jit_solution(12390189078183301018)
XLA Ops:
  0.6 53.9 %shard_map.147 = (bf16[576,512]{1,0:T(8,128)(2,1)}, bf16[576,512]{1,0:T(8,128)(2,1)}, f32[64,96]{1,0:T(8,128)}, f32[32,64]{1,0:T(8,128)}) custom-call(bf16[576,512]{1,0:T(8,128)(2,1)} %bitcast.7, bf16[576,512]{1,0:T(8,128)(2,1)} %bitcast.8, s32[6,4,24]{2,1,0:T(4,128)} %bitcast.12, f32[1,512]{1,0:T(1,128)} %bitcast.13, bf16[512,1536]{1,0:T(8,128)(2,1)} %w_hbm.1, ...), custom_call_target="tpu_custom_call" | custom-call | flops 6000000000 | bytes 10000000 | tf_op jit(solution)/shard_map/pallas_call | solution.py:426
  54.5 2.3 %shard_map.148 = (bf16[576,512]{1,0:T(8,128)(2,1)}, bf16[576,512]{1,0:T(8,128)(2,1)}, f32[64,96]{1,0:T(8,128)}, f32[32,64]{1,0:T(8,128)}) custom-call(bf16[576,512]{1,0:T(8,128)(2,1)} %get-tuple-element.12.refs_0_, bf16[576,512]{1,0:T(8,128)(2,1)} %get-tuple-element.13.refs_1_, f32[64,96]{1,0:T(8,128)} %get-tuple-element.14.refs_2_, ...), custom_call_target="tpu_custom_call" | custom-call | tf_op jit(solution)/shard_map/pallas_call | solution.py:462

commit v9 on v8

--- a/solution.py
+++ b/solution.py
@@ -252,7 +252,7 @@
             gp_ref[rows, pl.ds(col, 128)] = gq.astype(BF)
             gp_ref[rows, pl.ds(512 + col, 128)] = jnp.concatenate(gkt, 0).astype(BF).T
             gp_ref[rows, pl.ds(1024 + col, 128)] = jnp.concatenate(gvt, 0).astype(BF).T
-            if w == 1:
+            if w == 2:
                 z_sends.append(z_stage(p - 1 if p else 4))
 
     def group(g):

time: 57.2 us -> 57.8 us (1.010)
  Pallas kernels: 56.2 us -> 57 us
    pallas_call x1, Pallas kernels: 53.9 us -> 54.7 us  [on_device(): pl.pallas_call(kernel, out_shape=(jax.ShapeDtypeStruct((TOKENS, WIDTH), B...]
where the time goes in v9:
time: 57.8 us; the launch traced here: 57.6 us
  Pallas kernels  57 us (99%)
  between operations  0.64 us (1%)
    pallas_call x1, Pallas kernels, on_device(): pl.pallas_call(kernel, out_shape=(jax.ShapeDtypeStruct((TOKENS, WIDTH), B...  54.7 us
    pallas_call x1, Pallas kernels, on_device(): pl.pallas_call(hand_over, out_shape=tuple((jax.ShapeDtypeStruct(a.shape,...  2.3 us

profile of v9, /device:TPU:1, one launch (start us, length us, event | category | flops | bytes accessed | tf_op | source)
XLA Modules:
  0.0 57.6 jit_solution(7218797896484258647)
XLA Ops:
  0.6 54.7 %shard_map.147 = (bf16[576,512]{1,0:T(8,128)(2,1)}, bf16[576,512]{1,0:T(8,128)(2,1)}, f32[64,96]{1,0:T(8,128)}, f32[32,64]{1,0:T(8,128)}) custom-call(bf16[576,512]{1,0:T(8,128)(2,1)} %bitcast.7, bf16[576,512]{1,0:T(8,128)(2,1)} %bitcast.8, s32[6,4,24]{2,1,0:T(4,128)} %bitcast.12, f32[1,512]{1,0:T(1,128)} %bitcast.13, bf16[512,1536]{1,0:T(8,128)(2,1)} %w_hbm.1, ...), custom_call_target="tpu_custom_call" | custom-call | flops 6000000000 | bytes 10000000 | tf_op jit(solution)/shard_map/pallas_call | solution.py:426
  55.3 2.3 %shard_map.148 = (bf16[576,512]{1,0:T(8,128)(2,1)}, bf16[576,512]{1,0:T(8,128)(2,1)}, f32[64,96]{1,0:T(8,128)}, f32[32,64]{1,0:T(8,128)}) custom-call(bf16[576,512]{1,0:T(8,128)(2,1)} %get-tuple-element.12.refs_0_, bf16[576,512]{1,0:T(8,128)(2,1)} %get-tuple-element.13.refs_1_, f32[64,96]{1,0:T(8,128)} %get-tuple-element.14.refs_2_, ...), custom_call_target="tpu_custom_call" | custom-call | tf_op jit(solution)/shard_map/pallas_call | solution.py:462
